TPU v7x, 32 devices: a whole 2x2x4 slice. The times are simulated.
32 devices in a mesh: dp: 16 (over z, x, core), seq: 2 (over y).
Axes of the slice: x: 2, y: 2, z: 4, core: 2. Of those that a mesh axis runs over, the one named last changes fastest.
Arguments:
- pixels: bfloat16 [14336, 6912], P(('dp', 'seq')), may hold values from -6 to 6
- patch_size: int32 [64], P('dp'), may hold values from 12 to 48, as said below
- rows_first: int32 [64], P('dp'), may hold values from 2 to 12, as said below
- kernel_resize: bfloat16 [49, 48, 32], replicated, may hold values from -1.25 to 1.25
- pos_resize: float32 [31, 31, 7], replicated, may hold values from -2 to 2
- base_kernel: bfloat16 [3072, 768], P(None, 'dp'), may hold values from -0.109375 to 0.109375
- embed_bias: float32 [768], replicated, may hold values from -1.5 to 1.5
- pos_grid: bfloat16 [49, 768], P(None, 'dp'), may hold values from -3 to 3
- norm1_gain: float32 [768], replicated, may hold values from 0.25 to 1.75
- norm1_bias: float32 [768], replicated, may hold values from -1.5 to 1.5
- qkv_weight: bfloat16 [768, 2304], P(None, 'dp'), may hold values from -0.21875 to 0.21875
- query_bias: float32 [768], replicated, may hold values from -1.5 to 1.5
- value_bias: float32 [768], replicated, may hold values from -1.5 to 1.5
- proj_weight: bfloat16 [768, 768], P(None, 'dp'), may hold values from -0.875 to 0.875
- proj_bias: float32 [768], replicated, may hold values from -1.5 to 1.5
- norm2_gain: float32 [768], replicated, may hold values from 0.25 to 1.75
- norm2_bias: float32 [768], replicated, may hold values from -1.5 to 1.5
- fc1_weight: bfloat16 [768, 3072], P(None, 'dp'), may hold values from -0.21875 to 0.21875
- fc1_bias: float32 [3072], replicated, may hold values from -1.5 to 1.5
- fc2_weight: bfloat16 [3072, 768], P(None, 'dp'), may hold values from -0.109375 to 0.109375
- fc2_bias: float32 [768], replicated, may hold values from -1.5 to 1.5
- cotangent: bfloat16 [14336, 768], P(('dp', 'seq')), may hold values from -6 to 6
Outputs:
- block_out: bfloat16 [14336, 768], P(('dp', 'seq'))
- pixel_grad: bfloat16 [14336, 6912], P(('dp', 'seq'))
- grad_base_kernel: float32 [3072, 768], replicated
- grad_embed_bias: float32 [768], replicated
- grad_pos_grid: float32 [49, 768], replicated
- grad_norm1_gain: float32 [768], replicated
- grad_norm1_bias: float32 [768], replicated
- grad_qkv_weight: float32 [768, 2304], replicated
- grad_query_bias: float32 [768], replicated
- grad_value_bias: float32 [768], replicated
- grad_proj_weight: float32 [768, 768], replicated
- grad_proj_bias: float32 [768], replicated
- grad_norm2_gain: float32 [768], replicated
- grad_norm2_bias: float32 [768], replicated
- grad_fc1_weight: float32 [768, 3072], replicated
- grad_fc1_bias: float32 [3072], replicated
- grad_fc2_weight: float32 [3072, 768], replicated
- grad_fc2_bias: float32 [768], replicated
Inputs may be any that keep to these rules, and one draw needn't show every extreme that they name: `patch_size`: of the 4 images of each dp index, one, at a place drawn from the seed, has a patch side from 12 to 16 and rows on both seq indices; the others have patch sides from 24 to 48. For an image of grid side G, rows_first lies from G * 2 // 5 to G - G * 2 // 5. The tokens of one device never exceed 448.
All inputs are finite; a program needn't handle non-finite values.
Results may differ from a plain program's by a relative error of at most 0.018.
Values may be sent and summed in bfloat16 or wider, within the bound.
A program may use at most 256 MiB of HBM per device.

v0:
```python
import jax
import jax.numpy as jnp
from jax import lax
from jax.sharding import PartitionSpec as P

HEADS = 12
HEAD_DIM = 64
BASE = 32
GRID = 7
PMAX = 48
IMG_SIDE = 240
GTAB = 31


EPS = 1e-06
NEG = -1e30


def from_behind(value, axis, by):
    peers = lax.axis_size(axis)
    return lax.ppermute(value, axis, [(i, (i + by) % peers) for i in range(peers)])


def rounded(value):
    return lax.optimization_barrier(value.astype(jnp.bfloat16)).astype(jnp.float32)


def slot_info(patch_here, first_rows, seq_side, slot_total):
    grid_side = IMG_SIDE // patch_here
    row_total = jnp.where(seq_side == 0, first_rows, grid_side - first_rows)
    row_offset = jnp.where(seq_side == 0, 0, first_rows)
    filled = row_total * grid_side
    finish = jnp.cumsum(filled)
    starts = finish - filled
    slot_ids = jnp.arange(slot_total, dtype=jnp.int32)[:, None]
    member = ((slot_ids >= starts[None, :]) & (slot_ids < finish[None, :])).astype(jnp.int32)
    numbers = jnp.arange(patch_here.shape[0], dtype=jnp.int32)
    live_slot = jnp.sum(member, axis=1)
    image_ids = jnp.sum(member * numbers[None, :], axis=1) + live_slot - 1
    within = slot_ids[:, 0] - jnp.sum(member * starts[None, :], axis=1)
    grid_here = jnp.sum(member * grid_side[None, :], axis=1)
    patch_slot = jnp.sum(member * patch_here[None, :], axis=1)
    offset_here = jnp.sum(member * row_offset[None, :], axis=1)
    safe_grid = jnp.maximum(grid_here, 1)
    grid_row = jnp.where(live_slot > 0, within // safe_grid + offset_here, 0)
    grid_col = jnp.where(live_slot > 0, within % safe_grid, 0)
    return (image_ids, live_slot, patch_slot, grid_here, grid_row, grid_col)


def table_rows(lookup, rows_table):
    onehot = (lookup[:, None] == jnp.arange(rows_table.shape[0], dtype=jnp.int32)[None, :]).astype(
        jnp.float32
    )
    return jnp.dot(onehot, rows_table, precision=lax.Precision.HIGHEST)


def norm_parts(values_in):
    centred = values_in - jnp.mean(values_in, axis=-1, keepdims=True)
    inverse = lax.rsqrt(jnp.mean(centred * centred, axis=-1, keepdims=True) + EPS)
    return (centred * inverse, inverse)


def norm_back(grad_normed, normed, inverse):
    return inverse * (
        grad_normed
        - jnp.mean(grad_normed, axis=-1, keepdims=True)
        - normed * jnp.mean(grad_normed * normed, axis=-1, keepdims=True)
    )


def outer_sum(left, right):
    return lax.dot_general(
        left, right, (((0,), (0,)), ((), ())), preferred_element_type=jnp.float32
    )


def back_dot(left, right):
    return lax.dot_general(
        left, right, (((1,), (1,)), ((), ())), preferred_element_type=jnp.float32
    )


def gelu_exact(arguments):
    return jax.nn.gelu(arguments, approximate=False)


def body(
    pixels,
    patch_size,
    rows_first,
    kernel_resize,
    pos_resize,
    base_kernel,
    embed_bias,
    pos_grid,
    norm1_gain,
    norm1_bias,
    qkv_weight,
    query_bias,
    value_bias,
    proj_weight,
    proj_bias,
    norm2_gain,
    norm2_bias,
    fc1_weight,
    fc1_bias,
    fc2_weight,
    fc2_bias,
    cotangent,
):
    slot_total = pixels.shape[0]
    model_width = norm1_gain.shape[0]
    seq_side = lax.axis_index("seq")
    image_ids, live_slot, patch_slot, grid_here, grid_row, grid_col = slot_info(
        patch_size, rows_first, seq_side, slot_total
    )
    far_info = slot_info(patch_size, rows_first, 1 - seq_side, slot_total)
    key_ids = jnp.concatenate([image_ids, far_info[0]])
    key_live = jnp.concatenate([live_slot, far_info[1]])
    allowed = (image_ids[:, None] == key_ids[None, :]) & (key_live[None, :] > 0)
    live_rows = live_slot.astype(jnp.float32)[:, None]
    base_full, grid_full, qkv_full, proj_full, fc1_full, fc2_full = (
        lax.all_gather(base_kernel, "dp", axis=1, tiled=True),
        lax.all_gather(pos_grid, "dp", axis=1, tiled=True),
        lax.all_gather(qkv_weight, "dp", axis=1, tiled=True),
        lax.all_gather(proj_weight, "dp", axis=1, tiled=True),
        lax.all_gather(fc1_weight, "dp", axis=1, tiled=True),
        lax.all_gather(fc2_weight, "dp", axis=1, tiled=True),
    )
    kernel_flat = kernel_resize.reshape(PMAX + 1, PMAX * BASE).astype(jnp.float32)
    picked = table_rows(patch_slot, kernel_flat).reshape(slot_total, PMAX, BASE)
    inside = jnp.arange(PMAX, dtype=jnp.int32)[None, :, None] < patch_slot[:, None, None]
    resize = jnp.where(inside, picked, 0.0).astype(jnp.bfloat16)
    pos_flat = pos_resize.reshape(GTAB * GTAB, GRID)
    row_weight = table_rows(grid_here * GTAB + grid_row, pos_flat)
    col_weight = table_rows(grid_here * GTAB + grid_col, pos_flat)
    pos_weight = (
        (row_weight[:, :, None] * col_weight[:, None, :])
        .reshape(slot_total, GRID * GRID)
        .astype(jnp.bfloat16)
    )
    picture = pixels.reshape(slot_total, 3, PMAX, PMAX)
    partial_resize = jnp.einsum(
        "ncij,njb->ncib", picture, resize, preferred_element_type=jnp.float32
    ).astype(jnp.bfloat16)
    patches = (
        jnp.einsum("ncib,nia->ncab", partial_resize, resize, preferred_element_type=jnp.float32)
        .astype(jnp.bfloat16)
        .reshape(slot_total, 3 * BASE * BASE)
    )
    embed = (
        jnp.dot(patches, base_full, preferred_element_type=jnp.float32)
        + embed_bias
        + jnp.dot(pos_weight, grid_full, preferred_element_type=jnp.float32)
    )
    normed1, inverse1 = norm_parts(embed)
    hidden1 = (normed1 * norm1_gain + norm1_bias).astype(jnp.bfloat16)
    mixed = jnp.dot(hidden1, qkv_full, preferred_element_type=jnp.float32)
    head_shape = (slot_total, HEADS, HEAD_DIM)
    query_heads = (mixed[:, :model_width] + query_bias).astype(jnp.bfloat16).reshape(head_shape)
    key_heads = mixed[:, model_width : 2 * model_width].astype(jnp.bfloat16).reshape(head_shape)
    value_heads = (
        (mixed[:, 2 * model_width :] + value_bias).astype(jnp.bfloat16).reshape(head_shape)
    )
    far_keys, far_values = from_behind((key_heads, value_heads), "seq", 1)
    all_keys = jnp.concatenate([key_heads, far_keys], axis=0)
    all_values = jnp.concatenate([value_heads, far_values], axis=0)
    scale_factor = HEAD_DIM ** (-0.5)

    def attention_scores(keys_in):
        scores = (
            jnp.einsum("qhd,khd->hqk", query_heads, keys_in, preferred_element_type=jnp.float32)
            * scale_factor
        )
        return jnp.where(allowed[None], scores, NEG)

    scores = attention_scores(all_keys)
    row_max = jnp.max(scores, axis=-1, keepdims=True)
    exponent = jnp.exp(scores - row_max)
    row_total = jnp.sum(exponent, axis=-1, keepdims=True)
    attn_probs = exponent / row_total
    log_total = row_max + jnp.log(row_total)
    attended = (
        jnp.einsum(
            "hqk,khd->qhd",
            attn_probs.astype(jnp.bfloat16),
            all_values,
            preferred_element_type=jnp.float32,
        )
        .astype(jnp.bfloat16)
        .reshape(slot_total, model_width)
    )
    branch = jnp.dot(attended, proj_full, preferred_element_type=jnp.float32) + proj_bias
    middle = embed + branch
    normed2, inverse2 = norm_parts(middle)
    hidden2 = (normed2 * norm2_gain + norm2_bias).astype(jnp.bfloat16)
    pre_act = jnp.dot(hidden2, fc1_full, preferred_element_type=jnp.float32) + fc1_bias
    activated, gelu_back = jax.vjp(gelu_exact, pre_act)
    act_low = activated.astype(jnp.bfloat16)
    out_branch = jnp.dot(act_low, fc2_full, preferred_element_type=jnp.float32) + fc2_bias
    block_out = ((middle + out_branch) * live_rows).astype(jnp.bfloat16)
    grad_out = cotangent.astype(jnp.float32) * live_rows
    grad_final = grad_out.astype(jnp.bfloat16)
    grad_fc2 = outer_sum(act_low, grad_final)
    grad_fc2_bias = jnp.sum(grad_final.astype(jnp.float32), axis=0)
    grad_act = back_dot(grad_final, fc2_full)
    grad_pre = gelu_back(grad_act)[0].astype(jnp.bfloat16)
    grad_fc1 = outer_sum(hidden2, grad_pre)
    grad_fc1_bias = jnp.sum(grad_pre.astype(jnp.float32), axis=0)
    grad_hidden2 = rounded(back_dot(grad_pre, fc1_full))
    grad_norm2_gain = jnp.sum(grad_hidden2 * normed2, axis=0)
    grad_norm2_bias = jnp.sum(grad_hidden2, axis=0)
    grad_middle = grad_out + norm_back(grad_hidden2 * norm2_gain, normed2, inverse2)
    grad_branch = grad_middle.astype(jnp.bfloat16)
    grad_proj = outer_sum(attended, grad_branch)
    grad_proj_bias = jnp.sum(grad_branch.astype(jnp.float32), axis=0)
    grad_attended = back_dot(grad_branch, proj_full).astype(jnp.bfloat16).reshape(head_shape)
    back_keys, back_values = (far_keys, far_values)
    keys_back = jnp.concatenate([key_heads, back_keys], axis=0)
    values_back = jnp.concatenate([value_heads, back_values], axis=0)
    probs_back = jnp.exp(attention_scores(keys_back) - log_total)
    grad_probs = jnp.einsum(
        "qhd,khd->hqk", grad_attended, values_back, preferred_element_type=jnp.float32
    )
    grad_scores = (
        probs_back * (grad_probs - jnp.sum(probs_back * grad_probs, axis=-1, keepdims=True))
    ).astype(jnp.bfloat16)
    grad_query = (
        jnp.einsum("hqk,khd->qhd", grad_scores, keys_back, preferred_element_type=jnp.float32)
        * scale_factor
    ).astype(jnp.bfloat16)
    grad_keys_all = (
        jnp.einsum("hqk,qhd->khd", grad_scores, query_heads, preferred_element_type=jnp.float32)
        * scale_factor
    )
    grad_values_all = jnp.einsum(
        "hqk,qhd->khd",
        probs_back.astype(jnp.bfloat16),
        grad_attended,
        preferred_element_type=jnp.float32,
    )
    far_grad_keys, far_grad_values = (
        from_behind(grad_keys_all[slot_total:].astype(jnp.bfloat16), "seq", -1).astype(jnp.float32),
        from_behind(grad_values_all[slot_total:].astype(jnp.bfloat16), "seq", -1).astype(
            jnp.float32
        ),
    )
    grad_key_heads = (grad_keys_all[:slot_total] + far_grad_keys).astype(jnp.bfloat16)
    grad_value_heads = (grad_values_all[:slot_total] + far_grad_values).astype(jnp.bfloat16)
    grad_query_flat = grad_query.reshape(slot_total, model_width)
    grad_value_flat = grad_value_heads.reshape(slot_total, model_width)
    grad_mixed = jnp.concatenate(
        [grad_query_flat, grad_key_heads.reshape(slot_total, model_width), grad_value_flat], axis=1
    )
    grad_qkv = outer_sum(hidden1, grad_mixed)
    grad_query_bias = jnp.sum(grad_query_flat.astype(jnp.float32), axis=0)
    grad_value_bias = jnp.sum(grad_value_flat.astype(jnp.float32), axis=0)
    grad_hidden1 = rounded(back_dot(grad_mixed, qkv_full))
    grad_norm1_gain = jnp.sum(grad_hidden1 * normed1, axis=0)
    grad_norm1_bias = jnp.sum(grad_hidden1, axis=0)
    grad_embed = (grad_middle + norm_back(grad_hidden1 * norm1_gain, normed1, inverse1)).astype(
        jnp.bfloat16
    )
    grad_base = outer_sum(patches, grad_embed)
    grad_embed_bias = jnp.sum(grad_embed.astype(jnp.float32), axis=0)
    grad_pos = outer_sum(pos_weight, grad_embed)
    grad_patches = (
        back_dot(grad_embed, base_full).astype(jnp.bfloat16).reshape(slot_total, 3, BASE, BASE)
    )
    grad_partial = jnp.einsum(
        "ncab,nia->ncib", grad_patches, resize, preferred_element_type=jnp.float32
    ).astype(jnp.bfloat16)
    pixel_grad = (
        jnp.einsum("ncib,njb->ncij", grad_partial, resize, preferred_element_type=jnp.float32)
        .reshape(slot_total, 3 * PMAX * PMAX)
        .astype(jnp.bfloat16)
    )
    members = [
        grad_base,
        grad_embed_bias,
        grad_pos,
        grad_norm1_gain,
        grad_norm1_bias,
        grad_qkv,
        grad_query_bias,
        grad_value_bias,
        grad_proj,
        grad_proj_bias,
        grad_norm2_gain,
        grad_norm2_bias,
        grad_fc1,
        grad_fc1_bias,
        grad_fc2,
        grad_fc2_bias,
    ]
    stacked = jnp.concatenate([member.reshape(-1, model_width) for member in members], axis=0)
    summed = lax.psum(stacked, ("dp", "seq"))
    outputs = []
    position = 0
    for member in members:
        rows_here = member.size // model_width
        outputs.append(summed[position : position + rows_here].reshape(member.shape))
        position += rows_here
    return (
        block_out,
        pixel_grad,
        outputs[0],
        outputs[1],
        outputs[2],
        outputs[3],
        outputs[4],
        outputs[5],
        outputs[6],
        outputs[7],
        outputs[8],
        outputs[9],
        outputs[10],
        outputs[11],
        outputs[12],
        outputs[13],
        outputs[14],
        outputs[15],
    )


def solution(mesh):
    in_specs = (
        P(("dp", "seq"), None),
        P("dp"),
        P("dp"),
        P(),
        P(),
        P(None, "dp"),
        P(),
        P(None, "dp"),
        P(),
        P(),
        P(None, "dp"),
        P(),
        P(),
        P(None, "dp"),
        P(),
        P(),
        P(),
        P(None, "dp"),
        P(),
        P(None, "dp"),
        P(),
        P(("dp", "seq"), None),
    )
    out_specs = (
        P(("dp", "seq"), None),
        P(("dp", "seq"), None),
        P(),
        P(),
        P(),
        P(),
        P(),
        P(),
        P(),
        P(),
        P(),
        P(),
        P(),
        P(),
        P(),
        P(),
        P(),
        P(),
    )
    return jax.shard_map(body, mesh=mesh, in_specs=in_specs, out_specs=out_specs, check_vma=False)
```

profile of v0, /device:TPU:1, one launch (start us, length us, event | category | flops | bytes accessed | tf_op | source)
XLA Modules:
  0.0 1102.7 jit_solution(15715968916587141400)
XLA Ops:
  14.1 1.4 convert_reduce_fusion.8
  18.4 25.4 %all_gather.19 = bf16[49,768]{0,1:T(8,128)(2,1)} all-gather(bf16[49,48]{0,1:T(8,128)(2,1)} %param.29), channel_id=1, replica_groups=mesh['dp'=16,'seq'=2] {'dp'}, dimensions={1}, use_global_device_ids=true | all-gather | bytes 79968 | tf_op jit(solution)/shard_map/all_gather | solution.py:124
  44.4 3.6 copy.81
  48.1 9.4 copy.65
  57.5 17.8 %copy.67 = bf16[448,3,48,48]{3,2,1,0:T(8,128)(2,1)} copy(bf16[448,3,48,48]{0,3,2,1:T(8,128)(2,1)} %bitcast.102) | data formatting | bytes 12386304 | tf_op jit(solution)/shard_map/reshape | solution.py:142
  75.2 32.0 %convert_bitcast_fusion = bf16[448,3,32,32]{3,2,1,0:T(8,128)(2,1)} fusion(bf16[448,48,32,1]{1,2,3,0:T(8,128)(2,1)} %copy.81, bf16[448,3,48,48]{3,2,1,0:T(8,128)(2,1)} %copy.67), kind=kOutput, calls=%fused_computation.13 | convolution fusion | flops 333742080 | bytes 10321920 | tf_op jit(solution)/shard_map/ncib,nia->ncab/dot_general | solution.py:147
  107.2 11.6 %copy.69 = bf16[448,3,32,32]{0,3,2,1:T(8,128)(2,1)S(1)} copy(bf16[448,3,32,32]{3,2,1,0:T(8,128)(2,1)} %convert_bitcast_fusion) | data formatting | bytes 5505024 | tf_op jit(solution)/shard_map/convert_element_type | solution.py:148
  118.9 1.6 copy-done.19
  120.5 5.2 fusion.101
  126.6 4.0 fusion.89
  130.7 2.0 copy-done.23
  133.0 1.3 collective-permute-start.1
  134.8 3.0 fusion.52
  137.9 1.4 copy.71
  139.2 2.6 copy.70
  142.0 10.0 collective-permute-done.1
  152.9 5.8 fusion.99
  158.7 4.8 fusion
  163.5 5.4 collective-permute-done
  168.9 6.7 fusion.39
  175.7 2.9 fusion.100
  178.9 29.9 %all-gather.12.cloned.1.call-done = bf16[768,3072]{0,1:T(8,128)(2,1)} async-done(((bf16[768,192]{0,1:T(8,128)(2,1)}), bf16[768,3072]{0,1:T(8,128)(2,1)}) %all-gather.12.cloned.1.call-update) | async-done | bytes 4718608 | tf_op jit(solution)/shard_map/all_gather | solution.py:127
  208.9 18.0 %multiply_convert_fusion.1 = (bf16[448,3072]{1,0:T(8,128)(2,1)}, f32[448,3072]{1,0:T(8,128)}, f32[448,3072]{1,0:T(8,128)}) fusion(f32[3072]{0:T(1024)S(1)} %copy-done.47, bf16[768,3072]{0,1:T(8,128)(2,1)} %all-gather.12.cloned.1.call-done, f32[448,768]{1,0:T(8,128)S(1)} %get-tuple-element.109, f32[768]{0:T(1024)S(1)} %copy-done.48, f32[768]{0:T(1024)S(1)} %copy-done.37, ...), kind=kOutput, calls=%fused_computation.24 | convolution fusion | flops 2206482432 | bytes 19879424 | tf_op jit(solution)/shard_map/dot_general | solution.py:197
  226.8 36.1 %all-gather.14.cloned.1.call-done = bf16[3072,768]{0,1:T(8,128)(2,1)} async-done(((bf16[3072,48]{0,1:T(8,128)(2,1)}), bf16[3072,768]{0,1:T(8,128)(2,1)}) %all-gather.14.cloned.1.call-update) | async-done | bytes 4718608 | tf_op jit(solution)/shard_map/all_gather | solution.py:128
  262.9 9.9 convert_reduce_fusion
  272.9 5.9 fusion.90
  278.8 2.3 convolution_convert_fusion.3
  282.5 1.6 convolution_convert_fusion.1
  284.1 2.3 copy.73
  286.3 8.5 fusion.33
  294.9 1.5 copy-done.8
  298.9 12.8 %multiply_reduce_fusion = (f32[12,448]{1,0:T(8,128)S(1)}, f32[12,448,896]{2,1,0:T(8,128)}) fusion(f32[12,448,896]{2,1,0:T(8,128)} %copy-done.2, f32[12,448]{1,0:T(8,128)S(1)} %log_add_fusion, bf16[448,12,64]{0,2,1:T(8,128)(2,1)S(1)} %bitcast.110, bf16[448,12,64]{0,2,1:T(8,128)(2,1)} %collective-permute-done, bf16[448,12,64]{0,2,1:T(8,128)(2,1)S(1)} %bitcast.118), kind=kOutput, calls=%fused_computation.1 | convolution fusion | flops 633760512 | bytes 40642560 | tf_op jit(solution)/shard_map/qhd,khd->hqk/dot_general | solution.py:222
  311.7 13.4 %multiply_convert_fusion = bf16[12,448,896]{2,1,0:T(8,128)(2,1)S(1)} fusion(f32[12,448,896]{2,1,0:T(8,128)} %get-tuple-element.112, f32[12,448,896]{2,1,0:T(8,128)} %copy-done.2, f32[12,448]{1,0:T(8,128)S(1)} %get-tuple-element.111, f32[12,448]{1,0:T(8,128)S(1)} %log_add_fusion), kind=kLoop, calls=%fused_computation | loop fusion | flops 19267584 | bytes 48211968 | tf_op jit(solution)/shard_map/convert_element_type | solution.py:227
  325.1 1.7 multiply_bitcast_fusion
  326.7 1.6 slice.143
  328.6 3.9 convert_reduce_fusion.4
  332.5 8.3 fusion.83
  340.9 11.5 %reshape.439 = f32[3072,768]{1,0:T(8,128)} reshape(f32[768,3072]{1,0:T(8,128)} %fusion.90) | data formatting | bytes 18874368 | tf_op jit(solution)/shard_map/reshape | solution.py:296
  352.5 3.5 fusion.78
  356.0 1.6 convert_reduce_fusion.3
  357.6 1.4 fusion.37
  359.0 1.9 convolution_convert_fusion.2
  362.8 5.3 fusion.102
  368.4 5.3 fusion.54
  373.7 8.4 reshape.433
  382.2 104.4 %concatenate.29 = f32[12350,768]{1,0:T(8,128)} concatenate(f32[3072,768]{1,0:T(8,128)} %fusion.102, f32[1,768]{1,0:T(1,128)S(1)} %reshape.430, f32[49,768]{1,0:T(8,128)S(1)} %fusion.103, f32[1,768]{1,0:T(1,128)S(1)} %reshape.431, f32[1,768]{1,0:T(1,128)S(1)} %reshape.432, f32[2304,768]{1,0:T(8,128)} %reshape.433, f32[1,768]{1,0:T(1,128)S(1)} %reshape.434, ...), dimensions={0} | concatenate | bytes 75878400 | tf_op jit(solution)/shard_map/concatenate | solution.py:296
  486.7 1.4 copy-done.16
  488.1 3.4 copy.75
  491.4 7.1 multiply_convert_fusion.3
  498.5 6.4 convolution_convert_fusion
  504.9 3.1 copy.74
  508.0 10.4 copy.76
  518.4 14.7 %fusion.104 = f32[448,48,96]{1,2,0} fusion(bf16[448,32,96]{1,2,0:T(8,128)(2,1)} %bitcast.100, bf16[448,48,32]{1,2,0:T(8,128)(2,1)} %copy.75), kind=kOutput, calls=%fused_computation.197 | convolution fusion | flops 132120576 | bytes 12386304
  533.1 17.2 %fusion.10 = bf16[448,3,48,48]{3,2,1,0:T(8,128)(2,1)} fusion(bf16[448,48,32,1]{1,2,3,0:T(8,128)(2,1)S(1)} %copy-done.3, f32[448,48,3,32]{1,3,2,0:T(8,128)} %bitcast.99), kind=kOutput, calls=%fused_computation.16 | convolution fusion | flops 203341824 | bytes 15826944 | tf_op jit(solution)/shard_map/ncib,njb->ncij/dot_general | solution.py:274
  550.3 19.0 %copy.78 = bf16[448,3,48,48]{0,3,2,1:T(8,128)(2,1)} copy(bf16[448,3,48,48]{3,2,1,0:T(8,128)(2,1)} %fusion.10) | data formatting | bytes 12386304 | tf_op jit(solution)/shard_map/convert_element_type | solution.py:276
  569.3 9.6 copy.79
  578.9 462.2 %all-reduce.2.cloned.1.call-done = f32[12350,768]{1,0:T(8,128)} async-done(((f32[12350,768]{1,0:T(8,128)}), f32[12350,768]{1,0:T(8,128)}) %all-reduce.2.cloned.1.call-update) | async-done | bytes 37939216 | tf_op jit(solution)/shard_map/psum | solution.py:297
  1041.1 6.4 slice.107
  1047.6 8.6 reshape.445
  1056.2 19.9 %fusion.96 = (f32[3072,768]{1,0:T(8,128)}, f32[3072,768]{1,0:T(8,128)}, f32[3072,768]{1,0:T(8,128)}) fusion(f32[12350,768]{1,0:T(8,128)} %all-reduce.2.cloned.1.call-done), kind=kLoop, calls=%fused_computation.189 | loop fusion | bytes 56623104 | tf_op jit(solution)/shard_map/slice | solution.py:302
  1076.2 11.5 %reshape.451 = f32[768,3072]{1,0:T(8,128)} reshape(f32[3072,768]{1,0:T(8,128)} %get-tuple-element.92) | data formatting | bytes 18874368 | tf_op jit(solution)/shard_map/reshape | solution.py:302
  1089.0 1.6 slice_reduce_fusion
  1090.6 1.6 slice.104
  1092.2 3.2 slice.110
  (170 shorter events, 21.5 us)
Async XLA Ops:
  7.2 36.7 %copy-start = (bf16[49,48,32]{0,2,1:T(8,128)(2,1)S(1)}, bf16[49,48,32]{0,2,1:T(8,128)(2,1)}, u32[]{:S(2)}) copy-start(bf16[49,48,32]{0,2,1:T(8,128)(2,1)} %param.25) | copy-start | bytes 451588
  7.2 111.7 %all-gather.6.cloned.1.call-start = ((), (), s32[]{:S(2)}) async-start(), calls=%async_computation | async-start | bytes 5013504 | tf_op jit(solution)/shard_map/all_gather | solution.py:123
  7.9 118.7 %all-gather.8.cloned.1.call-start = ((), (), s32[]{:S(2)}) async-start(), calls=%async_computation.1 | async-start | bytes 3760128 | tf_op jit(solution)/shard_map/all_gather | solution.py:125
  8.7 167.0 %all-gather.10.cloned.1.call-start = ((), (), s32[]{:S(2)}) async-start(), calls=%async_computation.2 | async-start | bytes 1253376 | tf_op jit(solution)/shard_map/all_gather | solution.py:126
  9.4 199.4 %all-gather.12.cloned.1.call-start = ((), (), s32[]{:S(2)}) async-start(), calls=%async_computation.3 | async-start | bytes 5013504 | tf_op jit(solution)/shard_map/all_gather | solution.py:127
  10.0 252.9 %all-gather.14.cloned.1.call-start = ((), (), s32[]{:S(2)}) async-start(), calls=%async_computation.4 | async-start | bytes 5013504 | tf_op jit(solution)/shard_map/all_gather | solution.py:128
  10.6 1030.5 %all-reduce.2.cloned.1.call-start = ((), (), s32[]{:S(2)}) async-start(), calls=%async_computation.5 | async-start | bytes 75890688 | tf_op jit(solution)/shard_map/psum | solution.py:297
  44.4 13.0 %copy-start.15 = (bf16[448,48,32]{0,1,2:T(8,128)(2,1)}, bf16[448,48,32]{0,1,2:T(8,128)(2,1)S(1)}, u32[]{:S(2)}) copy-start(bf16[448,48,32]{0,1,2:T(8,128)(2,1)S(1)} %select_convert_fusion) | copy-start | bytes 4128772
  107.2 11.6 %copy-start.40 = (s32[448]{0:T(512)S(1)}, s32[448]{0:T(512)}, u32[]{:S(2)}) copy-start(s32[448]{0:T(512)} %get-tuple-element.78) | copy-start | bytes 5380
  118.8 1.6 copy-start.19
  120.5 5.2 copy-start.28
  120.5 5.2 copy-start.31
  120.5 5.2 copy-start.41
  125.7 0.9 copy-start.38
  125.7 0.9 copy-start.49
  126.2 4.4 copy-start.4
  126.2 4.4 copy-start.33
  126.5 4.1 copy-start.35
  126.5 8.2 copy-start.43
  126.6 8.2 copy-start.44
  130.7 2.0 copy-start.23
  133.0 8.8 copy-start.12
  133.0 19.0 %collective-permute-start.1 = (bf16[448,12,64]{0,2,1:T(8,128)(2,1)S(1)}, bf16[448,12,64]{0,2,1:T(8,128)(2,1)S(1)}, u32[]{:S(2)}, u32[]{:S(2)}) collective-permute-start(bf16[448,12,64]{0,2,1:T(8,128)(2,1)S(1)} %bitcast.106), channel_id=1, source_target_pairs={{0,1},{1,0},{2,3},{3,2},{4,5},{5,4},{6,7},{7,6},{8,9},{9,8},{10,11... | collective-permute-start | bytes 2064392 | tf_op jit(solution)/shard_map/ppermute | solution.py:21
  139.2 19.4 %copy-start.10 = (bf16[448,768]{0,1:T(8,128)(2,1)}, bf16[448,768]{0,1:T(8,128)(2,1)S(1)}, u32[]{:S(2)}) copy-start(bf16[448,768]{0,1:T(8,128)(2,1)S(1)} %copy.71) | copy-start | bytes 2064388
  141.8 27.1 %collective-permute-start = (bf16[448,12,64]{0,2,1:T(8,128)(2,1)}, bf16[448,12,64]{0,2,1:T(8,128)(2,1)}, u32[]{:S(2)}, u32[]{:S(2)}) collective-permute-start(bf16[448,12,64]{0,2,1:T(8,128)(2,1)} %bitcast.116), channel_id=1, source_target_pairs={{0,1},{1,0},{2,3},{3,2},{4,5},{5,4},{6,7},{7,6},{8,9},{9,8},{10,11... | collective-permute-start | bytes 2064392 | tf_op jit(solution)/shard_map/ppermute | solution.py:21
  152.0 0.9 copy-start.17
  158.7 10.2 copy-start.2
  163.5 12.1 %copy-start.42 = (f32[768]{0:T(1024)S(1)}, f32[768]{0:T(1024)}, u32[]{:S(2)}) copy-start(f32[768]{0:T(1024)} %param.36) | copy-start | bytes 9220
  175.6 51.3 %copy-start.21 = (bf16[12,64,448]{2,1,0:T(8,128)(2,1)}, bf16[12,64,448]{2,1,0:T(8,128)(2,1)S(1)}, u32[]{:S(2)}) copy-start(bf16[12,64,448]{2,1,0:T(8,128)(2,1)S(1)} %fusion.39) | copy-start | bytes 2064388
  175.6 33.3 %copy-start.37 = (f32[768]{0:T(1024)S(1)}, f32[768]{0:T(1024)}, u32[]{:S(2)}) copy-start(f32[768]{0:T(1024)} %param.37) | copy-start | bytes 9220
  175.6 33.3 %copy-start.47 = (f32[3072]{0:T(1024)S(1)}, f32[3072]{0:T(1024)}, u32[]{:S(2)}) copy-start(f32[3072]{0:T(1024)} %param.40) | copy-start | bytes 36868
  175.6 33.2 %copy-start.48 = (f32[768]{0:T(1024)S(1)}, f32[768]{0:T(1024)}, u32[]{:S(2)}) copy-start(f32[768]{0:T(1024)} %param.38) | copy-start | bytes 9220
  272.8 5.9 copy-start.45
  278.7 3.0 copy-start.29
  281.1 1.4 copy-start.26
  286.3 12.5 %copy-start.14 = (bf16[448,768]{0,1:T(8,128)(2,1)S(1)}, bf16[448,768]{0,1:T(8,128)(2,1)}, u32[]{:S(2)}) copy-start(bf16[448,768]{0,1:T(8,128)(2,1)} %copy.73) | copy-start | bytes 2064388
  286.3 12.5 %copy-start.22 = (bf16[448,768]{0,1:T(8,128)(2,1)S(1)}, bf16[448,768]{0,1:T(8,128)(2,1)}, u32[]{:S(2)}) copy-start(bf16[448,768]{0,1:T(8,128)(2,1)} %copy.70) | copy-start | bytes 2064388
  294.9 1.5 copy-start.8
  297.7 58.3 %collective-permute-start.3 = (bf16[448,12,64]{0,2,1:T(8,128)(2,1)}, bf16[448,12,64]{0,2,1:T(8,128)(2,1)}, u32[]{:S(2)}, u32[]{:S(2)}) collective-permute-start(bf16[448,12,64]{0,2,1:T(8,128)(2,1)} %slice.142), channel_id=1, source_target_pairs={{0,1},{1,0},{2,3},{3,2},{4,5},{5,4},{6,7},{7,6},{8,9},{9,8},{10,11... | collective-permute-start | bytes 2064392 | tf_op jit(solution)/shard_map/ppermute | solution.py:21
  311.7 13.4 %copy-start.11 = (bf16[448,768]{0,1:T(8,128)(2,1)S(1)}, bf16[448,768]{0,1:T(8,128)(2,1)}, u32[]{:S(2)}) copy-start(bf16[448,768]{0,1:T(8,128)(2,1)} %copy-done.10) | copy-start | bytes 2064388
  325.0 3.6 copy-start.13
  325.0 3.5 copy-start.18
  326.7 5.8 copy-start.6
  328.3 4.2 copy-start.30
  328.3 29.2 %collective-permute-start.2 = (bf16[448,12,64]{0,2,1:T(8,128)(2,1)}, bf16[448,12,64]{0,2,1:T(8,128)(2,1)}, u32[]{:S(2)}, u32[]{:S(2)}) collective-permute-start(bf16[448,12,64]{0,2,1:T(8,128)(2,1)} %slice.143), channel_id=1, source_target_pairs={{0,1},{1,0},{2,3},{3,2},{4,5},{5,4},{6,7},{7,6},{8,9},{9,8},{10,11... | collective-permute-start | bytes 2064392 | tf_op jit(solution)/shard_map/ppermute | solution.py:21
  352.5 3.5 copy-start.9
  352.5 5.1 copy-start.7
  356.0 3.0 copy-start.27
  356.0 3.0 copy-start.46
  359.0 1.9 copy-start.5
  359.0 1.9 copy-start.34
  359.0 1.9 copy-start.36
  359.0 1.9 copy-start.39
  360.9 1.9 copy-start.20
  362.2 5.9 copy-start.24
  362.8 5.3 copy-start.32
  362.8 5.6 copy-start.50
  486.6 1.4 copy-start.16
  488.0 3.4 copy-start.51
  491.4 7.1 copy-start.25
  518.4 14.7 %copy-start.3 = (bf16[448,48,32,1]{1,2,3,0:T(8,128)(2,1)S(1)}, bf16[448,48,32,1]{1,2,3,0:T(8,128)(2,1)}, u32[]{:S(2)}) copy-start(bf16[448,48,32,1]{1,2,3,0:T(8,128)(2,1)} %copy.81) | copy-start | bytes 4128772
  1076.2 19.3 %copy-start.1 = (bf16[49,48,32]{0,2,1:T(8,128)(2,1)S(1)}, bf16[49,48,32]{0,2,1:T(8,128)(2,1)}, u32[]{:S(2)}) copy-start(bf16[49,48,32]{0,2,1:T(8,128)(2,1)} %param.25) | copy-start | bytes 451588
Sparse Core Ops, SparseCore 0:
  10.3 56.2 all-gather.5
  68.9 45.7 all-gather.7
  116.9 37.4 all-gather.9
  156.5 52.2 all-gather.11
  211.0 51.9 all-gather.13
  486.8 554.2 all-reduce.1
where the time goes:
time: 1120 us; the launch traced here: 1100 us
  waiting for transfers between devices  547 us (49%)
  local copies, waits for them, and re-layouts  286 us (26%)
  matrix products  194 us (17%)
  other arithmetic  32.1 us (3%)
  blocking collectives  25.4 us (2%)
  between operations  15.4 us (1%)
    psum x1, waiting for transfers between devices, body(): summed = lax.psum(stacked, ('dp', 'seq'))  462 us
    concatenate x1, local copies, waits for them, and re-layouts, body(): jnp.concatenate([member.reshape(-1, model_width) for member in members],...  104 us
    all_gather x1, waiting for transfers between devices, body(): lax.all_gather(fc2_weight, 'dp', axis=1, tiled=True)  36.1 us
    slice x6, local copies, waits for them, and re-layouts, body(): outputs.append(summed[position:position + rows_here].reshape(member.shape))  33.5 us
    dot_general x1, matrix products, body(): jnp.einsum('ncib,nia->ncab', partial_resize, resize, preferred_element_ty...  32 us
    all_gather x1, waiting for transfers between devices, body(): lax.all_gather(fc1_weight, 'dp', axis=1, tiled=True)  29.9 us
    dot_general x6, matrix products, outer_sum(): lax.dot_general(left, right, (((0,), (0,)), ((), ())), preferred_element_...  28.5 us
    unnamed x106, local copies, waits for them, and re-layouts  27.2 us
  transfers between devices with their start and end apart: 10, of which 5 were waited for; matrix products, arithmetic and copies ran while one was open for 26% of the time, Pallas kernels for 0%

commit v1 on v0

--- a/solution.py
+++ b/solution.py
@@ -1,6 +1,10 @@
+import functools
+
 import jax
 import jax.numpy as jnp
 from jax import lax
+from jax.experimental import pallas as pl
+from jax.experimental.pallas import tpu as pltpu
 from jax.sharding import PartitionSpec as P
 
 HEADS = 12
@@ -10,6 +14,231 @@
 PMAX = 48
 IMG_SIDE = 240
 GTAB = 31
+
+
+MESH = pl.DeviceIdType.MESH
+
+
+def place():
+    me, y = lax.axis_index("dp"), lax.axis_index("seq")
+    core = lax.rem(me, 2)
+    x = lax.rem(me // 2, 2)
+    z = me // 4
+    return me, core, x, y, z
+
+
+def peers():
+    me, core, x, y, z = place()
+    sib = (me + 1 - 2 * core, y)
+    xn = (me + 2 - 4 * x, y)
+    yn = (me, 1 - y)
+    zn = [(lax.rem(z + k, 4) * 4 + x * 2 + core, y) for k in (1, 2, 3)]
+    return sib, xn, yn, zn
+
+
+def greet():
+    sib, xn, yn, zn = peers()
+    barrier = pltpu.get_barrier_semaphore()
+    for other in [sib, xn, yn] + zn:
+        pl.semaphore_signal(barrier, inc=1, device_id=other, device_id_type=MESH)
+    pl.semaphore_wait(barrier, 6)
+
+
+def add_rows(dst, src, rows, step):
+    def one(i, carry):
+        at = pl.ds(pl.multiple_of(i * step, step), step)
+        dst[at, :] = dst[at, :] + src[at, :]
+        return carry
+
+    lax.fori_loop(0, rows // step, one, 0)
+
+
+class Chunk:
+    def __init__(self, array, j, rq, col, h):
+        self.array, self.j, self.rq, self.col, self.h = array, j, rq, col, h
+
+
+def reduce_kernel(chunks, n_in, *refs):
+    ins, outs = refs[:n_in], refs[n_in : 2 * n_in]
+    rest = list(refs[2 * n_in :])
+    n = len(chunks)
+    send, recv, loc = rest[-3:]
+    bufs = [rest[i * 7 : i * 7 + 7] for i in range(n)]
+    me, core, x, y, z = place()
+    sib, xn, yn, zn = peers()
+    greet()
+    started = {}
+
+    def remote(w, number, src, dst, to):
+        cp = pltpu.make_async_remote_copy(
+            src_ref=src, dst_ref=dst, send_sem=send.at[w, number], recv_sem=recv.at[w, number],
+            device_id=to, device_id_type=MESH)
+        cp.start()
+        started[w, number] = cp
+
+    def stage(w, s):
+        c = chunks[w]
+        g, out = ins[c.array].at[c.j], outs[c.array].at[c.j]
+        own, acc, a1, b1, a2, b2, zz = bufs[w]
+        rq, h = c.rq, c.h
+        ha, rz = rq // 2, rq // 4
+        mine = pl.ds(pl.multiple_of(c.col + core * h, 128), h)
+        theirs = pl.ds(pl.multiple_of(c.col + (1 - core) * h, 128), h)
+        step = 96 if ha % 96 == 0 else 32
+        if s == 0:
+            remote(w, 0, g.at[:, :, :, theirs], acc, sib)
+            cp = pltpu.make_async_copy(g.at[:, :, :, mine], own, loc.at[w, 0])
+            cp.start()
+            started[w, "own"] = cp
+        if s == 1:
+            started[w, "own"].wait()
+            started[w, 0].wait_recv()
+            for i in range(2):
+                for k in range(2):
+                    add_rows(acc.at[i, k], own.at[i, k], rq, step)
+            remote(w, 1, acc.at[1 - x, :, pl.ds(0, ha), :], a1, xn)
+            remote(w, 2, acc.at[:, 1 - y, pl.ds(ha, ha), :], b1, yn)
+        if s == 2:
+            started[w, 1].wait_recv()
+            started[w, 2].wait_recv()
+            add_rows(acc.at[x, 1 - y, pl.ds(0, ha)], a1.at[1 - y], ha, step)
+            remote(w, 3, acc.at[x, 1 - y, pl.ds(0, ha), :], a2, yn)
+            add_rows(acc.at[1 - x, y, pl.ds(ha, ha)], b1.at[1 - x], ha, step)
+            remote(w, 4, acc.at[1 - x, y, pl.ds(ha, ha), :], b2, xn)
+            add_rows(acc.at[x, y, pl.ds(0, ha)], a1.at[y], ha, step)
+            add_rows(acc.at[x, y, pl.ds(ha, ha)], b1.at[x], ha, step)
+        if s == 3:
+            started[w, 3].wait_recv()
+            started[w, 4].wait_recv()
+            add_rows(acc.at[x, y, pl.ds(0, ha)], a2, ha, step)
+            add_rows(acc.at[x, y, pl.ds(ha, ha)], b2, ha, step)
+            for k in (1, 2, 3):
+                rows = pl.ds(pl.multiple_of(lax.rem(z + k, 4) * rz, 16), rz)
+                remote(w, 4 + k, acc.at[x, y, rows, :], zz.at[k - 1], zn[k - 1])
+        if s == 4:
+            for k in (1, 2, 3):
+                started[w, 4 + k].wait_recv()
+
+            def total(i, carry):
+                at = pl.ds(pl.multiple_of(i * 16, 16), 16)
+                here = pl.ds(pl.multiple_of(z * rz + i * 16, 16), 16)
+                f = lambda v: v.astype(jnp.float32)
+                both = f(acc[x, y, here, :]) + f(zz[0, at, :])
+                both = both + f(zz[1, at, :]) + f(zz[2, at, :])
+                zz[3, at, :] = both.astype(jnp.bfloat16)
+                return carry
+
+            lax.fori_loop(0, rz // 16, total, 0)
+            rows = pl.ds(pl.multiple_of(z * rz, 16), rz)
+            for k in (1, 2, 3):
+                remote(w, 7 + k, zz.at[3], out.at[x, y, rows, mine], zn[k - 1])
+            cp = pltpu.make_async_copy(zz.at[3], out.at[x, y, rows, mine], loc.at[w, 1])
+            cp.start()
+            started[w, "fin"] = cp
+        if s == 5:
+            started[w, "fin"].wait()
+            for k in (1, 2, 3):
+                started[w, 7 + k].wait_recv()
+            part = out.at[x, y, pl.ds(0, ha), mine]
+            remote(w, 11, part, part, yn)
+            part = out.at[x, y, pl.ds(ha, ha), mine]
+            remote(w, 12, part, part, xn)
+        if s == 6:
+            started[w, 11].wait_recv()
+            started[w, 12].wait_recv()
+            part = out.at[x, :, pl.ds(0, ha), mine]
+            remote(w, 13, part, part, xn)
+            part = out.at[:, y, pl.ds(ha, ha), mine]
+            remote(w, 14, part, part, yn)
+        if s == 7:
+            started[w, 13].wait_recv()
+            started[w, 14].wait_recv()
+            part = out.at[:, :, :, mine]
+            remote(w, 15, part, part, sib)
+        if s == 8:
+            started[w, 15].wait_recv()
+
+    for tick in range(n + 8):
+        for w in range(n):
+            if 0 <= tick - w <= 8:
+                stage(w, tick - w)
+    for w in range(n):
+        for number in range(16):
+            started[w, number].wait_send()
+
+
+def all_sum(arrays, chunks):
+    scratch = []
+    for c in chunks:
+        ha, rz = c.rq // 2, c.rq // 4
+        scratch += [
+            pltpu.VMEM((2, 2, c.rq, c.h), jnp.bfloat16),
+            pltpu.VMEM((2, 2, c.rq, c.h), jnp.bfloat16),
+            pltpu.VMEM((2, ha, c.h), jnp.bfloat16),
+            pltpu.VMEM((2, ha, c.h), jnp.bfloat16),
+            pltpu.VMEM((ha, c.h), jnp.bfloat16),
+            pltpu.VMEM((ha, c.h), jnp.bfloat16),
+            pltpu.VMEM((4, rz, c.h), jnp.bfloat16),
+        ]
+    n = len(chunks)
+    scratch += [
+        pltpu.SemaphoreType.DMA((n, 16)),
+        pltpu.SemaphoreType.DMA((n, 16)),
+        pltpu.SemaphoreType.DMA((n, 2)),
+    ]
+    return pl.pallas_call(
+        functools.partial(reduce_kernel, chunks, len(arrays)),
+        out_shape=[jax.ShapeDtypeStruct(a.shape, a.dtype) for a in arrays],
+        in_specs=[pl.BlockSpec(memory_space=pl.ANY)] * len(arrays),
+        out_specs=[pl.BlockSpec(memory_space=pl.ANY)] * len(arrays),
+        scratch_shapes=scratch,
+        compiler_params=pltpu.CompilerParams(
+            collective_id=1, has_side_effects=True, vmem_limit_bytes=60 * 2**20),
+    )(*arrays)
+
+
+CHUNKS = [
+    Chunk(0, 0, 384, 0, 384),
+    Chunk(0, 1, 384, 0, 384),
+    Chunk(1, 0, 192, 0, 768),
+    Chunk(1, 0, 192, 1536, 768),
+    Chunk(2, 0, 192, 0, 384),
+    Chunk(3, 0, 192, 0, 640),
+    Chunk(3, 0, 192, 1280, 512),
+    Chunk(4, 0, 384, 0, 384),
+    Chunk(4, 1, 384, 0, 384),
+    Chunk(5, 0, 64, 0, 384),
+]
+
+
+def summed_over_devices(large, small):
+    width = large[0].shape[1]
+    rows = jnp.concatenate([member.reshape(-1, width) for member in small], axis=0)
+    if lax.axis_size("dp") != 16 or lax.axis_size("seq") != 2:
+        large_sums = [
+            lax.psum(member.astype(jnp.bfloat16), ("dp", "seq")).astype(jnp.float32)
+            for member in large
+        ]
+        row_sums = lax.psum(rows, ("dp", "seq"))
+    else:
+        used = rows.shape[0]
+        rows = jnp.pad(rows, ((0, 256 - used), (0, 0)))
+        arrays = []
+        for member, parts in zip(large + [rows], (2, 1, 1, 1, 2, 1)):
+            quarter = member.shape[0] // (4 * parts)
+            arrays.append(
+                member.astype(jnp.bfloat16).reshape(parts, 2, 2, quarter, member.shape[1])
+            )
+        done = all_sum(arrays, CHUNKS)
+        large_sums = [d.reshape(m.shape).astype(jnp.float32) for d, m in zip(done, large)]
+        row_sums = done[-1].reshape(256, width)[:used].astype(jnp.float32)
+    small_sums = []
+    position = 0
+    for member in small:
+        count = member.size // width
+        small_sums.append(row_sums[position : position + count].reshape(member.shape))
+        position += count
+    return large_sums, small_sums
 
 
 EPS = 1e-06
@@ -275,7 +504,39 @@
         .reshape(slot_total, 3 * PMAX * PMAX)
         .astype(jnp.bfloat16)
     )
-    members = [
+    large, small = summed_over_devices(
+        [grad_fc2, grad_fc1, grad_proj, grad_qkv, grad_base],
+        [
+            grad_pos,
+            grad_embed_bias,
+            grad_norm1_gain,
+            grad_norm1_bias,
+            grad_query_bias,
+            grad_value_bias,
+            grad_proj_bias,
+            grad_norm2_gain,
+            grad_norm2_bias,
+            grad_fc1_bias,
+            grad_fc2_bias,
+        ],
+    )
+    grad_fc2, grad_fc1, grad_proj, grad_qkv, grad_base = large
+    (
+        grad_pos,
+        grad_embed_bias,
+        grad_norm1_gain,
+        grad_norm1_bias,
+        grad_query_bias,
+        grad_value_bias,
+        grad_proj_bias,
+        grad_norm2_gain,
+        grad_norm2_bias,
+        grad_fc1_bias,
+        grad_fc2_bias,
+    ) = small
+    return (
+        block_out,
+        pixel_grad,
         grad_base,
         grad_embed_bias,
         grad_pos,
@@ -292,34 +553,6 @@
         grad_fc1_bias,
         grad_fc2,
         grad_fc2_bias,
-    ]
-    stacked = jnp.concatenate([member.reshape(-1, model_width) for member in members], axis=0)
-    summed = lax.psum(stacked, ("dp", "seq"))
-    outputs = []
-    position = 0
-    for member in members:
-        rows_here = member.size // model_width
-        outputs.append(summed[position : position + rows_here].reshape(member.shape))
-        position += rows_here
-    return (
-        block_out,
-        pixel_grad,
-        outputs[0],
-        outputs[1],
-        outputs[2],
-        outputs[3],
-        outputs[4],
-        outputs[5],
-        outputs[6],
-        outputs[7],
-        outputs[8],
-        outputs[9],
-        outputs[10],
-        outputs[11],
-        outputs[12],
-        outputs[13],
-        outputs[14],
-        outputs[15],
     )
 
 

time: 1120 us -> 664 us (0.59)
  waiting for transfers between devices: 547 us -> 82.4 us
  local copies, waits for them, and re-layouts: 286 us -> 109 us
  Pallas kernels: 0 us -> 175 us
  other arithmetic: 32.1 us -> 57.6 us
    psum x1 -> x0, waiting for transfers between devices: 462 us -> none  [body(): summed = lax.psum(stacked, ('dp', 'seq'))]
    pallas_call x0 -> x1, Pallas kernels: none -> 175 us  [all_sum(): pl.pallas_call(functools.partial(reduce_kernel, chunks, len(arrays)), out...]
    concatenate x1, local copies, waits for them, and re-layouts: 104 us -> 0.08 us  [summed_over_devices(): jnp.concatenate([member.reshape(-1, width) for member in small], axis=0)]
    reshape x15 -> x11, local copies, waits for them, and re-layouts: 40.8 us -> 0.82 us  [the longest x1 0.61 us: summed_over_devices(): small_sums.append(row_sums[position:position + count].reshape(member.shape))]
    slice x6 -> x3, local copies, waits for them, and re-layouts: 33.5 us -> 1.35 us  [summed_over_devices(): small_sums.append(row_sums[position:position + count].reshape(member.shape))]
    convert_element_type x0 -> x6, other arithmetic: none -> 25.4 us  [the longest x5 24.5 us: summed_over_devices(): d.reshape(m.shape).astype(jnp.float32)]
    unnamed x106 -> x92, local copies, waits for them, and re-layouts: 27.2 us -> 24.4 us
  transfers between devices with their start and end apart: 10 -> 9, of which waited for: 5 -> 4; matrix products, arithmetic and copies ran while one was open for 26% -> 30% of each run, Pallas kernels for 0% -> 0%
where the time goes in v1:
time: 664 us; the launch traced here: 654 us
  matrix products  188 us (28%)
  Pallas kernels  175 us (26%)
  local copies, waits for them, and re-layouts  109 us (16%)
  waiting for transfers between devices  82.4 us (12%)
  other arithmetic  57.6 us (9%)
  blocking collectives  24 us (4%)
  between operations  15.1 us (2%)
    pallas_call x1, Pallas kernels, all_sum(): pl.pallas_call(functools.partial(reduce_kernel, chunks, len(arrays)), out...  175 us
    all_gather x1, waiting for transfers between devices, body(): lax.all_gather(fc2_weight, 'dp', axis=1, tiled=True)  36 us
    dot_general x1, matrix products, body(): jnp.einsum('ncib,nia->ncab', partial_resize, resize, preferred_element_ty...  32.1 us
    all_gather x1, waiting for transfers between devices, body(): lax.all_gather(fc1_weight, 'dp', axis=1, tiled=True)  28.6 us
    convert_element_type x5, other arithmetic, summed_over_devices(): d.reshape(m.shape).astype(jnp.float32)  24.5 us
    unnamed x92, local copies, waits for them, and re-layouts  24.4 us
    all_gather x1, blocking collectives, body(): lax.all_gather(pos_grid, 'dp', axis=1, tiled=True)  24 us
    dot_general x5, matrix products, back_dot(): lax.dot_general(left, right, (((1,), (1,)), ((), ())), preferred_element_...  21.8 us
  transfers between devices with their start and end apart: 9, of which 4 were waited for; matrix products, arithmetic and copies ran while one was open for 30% of the time, Pallas kernels for 0%

profile of v1, /device:TPU:1, one launch (start us, length us, event | category | flops | bytes accessed | tf_op | source)
XLA Modules:
  0.0 653.8 jit_solution(941085897164184291)
XLA Ops:
  10.6 1.0 reshape.452
  15.1 0.9 fusion.26
  16.1 1.0 fusion.25
  17.8 24.0 %all_gather.19 = bf16[49,768]{0,1:T(8,128)(2,1)S(1)} all-gather(bf16[49,48]{0,1:T(8,128)(2,1)} %param.29), channel_id=1, replica_groups=mesh['dp'=16,'seq'=2] {'dp'}, dimensions={1}, use_global_device_ids=true | all-gather | bytes 79968 | tf_op jit(solution)/shard_map/all_gather | solution.py:353
  42.4 3.4 copy.81
  45.8 9.5 %copy.65 = bf16[448,6912]{0,1:T(8,128)(2,1)} copy(bf16[448,6912]{1,0:T(8,128)(2,1)} %param.22) | data formatting | bytes 12386304 | tf_op args[0]
  55.3 17.8 %copy.67 = bf16[448,3,48,48]{3,2,1,0:T(8,128)(2,1)} copy(bf16[448,3,48,48]{0,3,2,1:T(8,128)(2,1)} %bitcast.124) | data formatting | bytes 12386304 | tf_op jit(solution)/shard_map/reshape | solution.py:371
  73.1 32.1 %convert_bitcast_fusion = bf16[448,3,32,32]{3,2,1,0:T(8,128)(2,1)} fusion(bf16[448,48,32,1]{1,2,3,0:T(8,128)(2,1)} %copy.81, bf16[448,3,48,48]{3,2,1,0:T(8,128)(2,1)} %copy.67), kind=kOutput, calls=%fused_computation.13 | convolution fusion | flops 333742080 | bytes 10321920 | tf_op jit(solution)/shard_map/ncib,nia->ncab/dot_general | solution.py:376
  105.3 12.8 %copy.69 = bf16[448,3,32,32]{0,3,2,1:T(8,128)(2,1)} copy(bf16[448,3,32,32]{3,2,1,0:T(8,128)(2,1)} %convert_bitcast_fusion) | data formatting | bytes 5505024 | tf_op jit(solution)/shard_map/convert_element_type | solution.py:377
  118.1 6.1 fusion.100
  125.2 4.0 fusion.87
  129.2 2.0 copy-done.16
  131.2 0.9 slice.125
  132.1 1.4 copy.72
  133.6 1.2 collective-permute-start.1
  134.8 3.4 copy.75
  138.6 3.0 fusion.52
  141.6 1.4 copy.71
  143.0 1.2 copy.70
  144.3 8.4 %collective-permute-done.1 = bf16[448,12,64]{0,2,1:T(8,128)(2,1)} collective-permute-done((bf16[448,12,64]{0,2,1:T(8,128)(2,1)S(1)}, bf16[448,12,64]{0,2,1:T(8,128)(2,1)}, u32[]{:S(2)}, u32[]{:S(2)}) %collective-permute-start.1) | collective-permute-done | bytes 688160 | tf_op jit(solution)/shard_map/ppermute | solution.py:250
  152.7 5.8 fusion.97
  158.5 4.8 fusion
  163.3 6.2 collective-permute-done
  169.6 7.3 %fusion.39 = bf16[12,64,448]{2,1,0:T(8,128)(2,1)} fusion(f32[12,448,896]{2,1,0:T(8,128)S(1)} %get-tuple-element.116, f32[12,448]{1,0:T(8,128)S(1)} %fusion, f32[12,448]{1,0:T(8,128)S(1)} %get-tuple-element.115, bf16[448,12,64]{0,2,1:T(8,128)(2,1)} %collective-permute-done, bf16[448,12,64]{0,2,1:T(8,128)(2,1)} %bitcast.12), kind=kOutput, calls=%fused_computation.76 | convolution fusion | flops 634109952 | bytes 21374976 | tf_op jit(solution)/shard_map/hqk,khd->qhd/dot_general | solution.py:413
  177.0 2.9 fusion.98
  180.2 28.6 %all-gather.12.cloned.1.call-done = bf16[768,3072]{0,1:T(8,128)(2,1)} async-done(((bf16[768,192]{0,1:T(8,128)(2,1)}), bf16[768,3072]{0,1:T(8,128)(2,1)}) %all-gather.12.cloned.1.call-update) | async-done | bytes 4718608 | tf_op jit(solution)/shard_map/all_gather | solution.py:356
  208.8 18.0 %multiply_convert_fusion.1 = (bf16[448,3072]{1,0:T(8,128)(2,1)}, f32[448,3072]{1,0:T(8,128)}, f32[448,3072]{1,0:T(8,128)}) fusion(f32[3072]{0:T(1024)S(1)} %copy-done.37, bf16[768,3072]{0,1:T(8,128)(2,1)} %all-gather.12.cloned.1.call-done, f32[448,768]{1,0:T(8,128)S(1)} %get-tuple-element.118, f32[768]{0:T(1024)S(1)} %copy-done.38, f32[768]{0:T(1024)S(1)} %copy-done.28, ...), kind=kOutput, calls=%fused_computation.23 | convolution fusion | flops 2206482432 | bytes 19879424 | tf_op jit(solution)/shard_map/dot_general | solution.py:426
  226.8 36.0 %all-gather.14.cloned.1.call-done = bf16[3072,768]{0,1:T(8,128)(2,1)} async-done(((bf16[3072,48]{0,1:T(8,128)(2,1)}), bf16[3072,768]{0,1:T(8,128)(2,1)}) %all-gather.14.cloned.1.call-update) | async-done | bytes 4718608 | tf_op jit(solution)/shard_map/all_gather | solution.py:357
  262.7 9.9 %fusion.99 = (bf16[3072]{0:T(1024)(128)(2,1)S(1)}, bf16[448,3072]{1,0:T(8,128)(2,1)S(1)}) fusion(f32[448,3072]{1,0:T(8,128)} %get-tuple-element.96, bf16[3072,768]{0,1:T(8,128)(2,1)} %all-gather.14.cloned.1.call-done, bf16[448,768]{1,0:T(8,128)(2,1)} %param.43, f32[448]{0:T(512)S(1)} %get-tuple-element.106, f32[448,3072]{1,0:T(8,128)} %get-tuple-element.119, ...), kind=kOutput, calls=%fused_computation.198 | convolution fusion | flops 2136978432 | bytes 19189504 | tf_op jit(solution)/shard_map/dot_general | solution.py:307
  272.6 5.1 convolution_convert_fusion
  277.7 2.3 convolution_convert_fusion.8
  281.7 1.1 copy-done.12
  282.8 1.6 convolution_convert_fusion.6
  284.3 2.3 copy.73
  286.6 8.5 %fusion.27 = f32[896,12,64]{0,2,1:T(8,128)S(1)} fusion(bf16[448,12,64]{0,2,1:T(8,128)(2,1)} %bitcast.131, f32[12,448,896]{2,1,0:T(8,128)} %copy-done.2, f32[12,448]{1,0:T(8,128)S(1)} %log_add_fusion), kind=kOutput, calls=%fused_computation.53 | convolution fusion | flops 626196480 | bytes 22729728 | tf_op jit(solution)/shard_map/hqk,qhd->khd/dot_general | solution.py:465
  295.1 1.5 copy-done.8
  296.6 1.2 slice.123
  297.8 1.2 collective-permute-start.3
  299.0 13.0 %multiply_reduce_fusion = (f32[12,448]{1,0:T(8,128)S(1)}, f32[12,448,896]{2,1,0:T(8,128)}) fusion(f32[12,448,896]{2,1,0:T(8,128)} %copy-done.2, f32[12,448]{1,0:T(8,128)S(1)} %log_add_fusion, bf16[448,12,64]{0,2,1:T(8,128)(2,1)S(1)} %bitcast.132, bf16[448,12,64]{0,2,1:T(8,128)(2,1)} %collective-permute-done, bf16[448,12,64]{0,2,1:T(8,128)(2,1)} %bitcast.12), kind=kOutput, calls=%fused_computation.1 | convolution fusion | flops 633760512 | bytes 40642560 | tf_op jit(solution)/shard_map/qhd,khd->hqk/dot_general | solution.py:451
  312.0 13.3 %multiply_convert_fusion = bf16[12,448,896]{2,1,0:T(8,128)(2,1)S(1)} fusion(f32[12,448,896]{2,1,0:T(8,128)} %get-tuple-element.121, f32[12,448,896]{2,1,0:T(8,128)} %copy-done.2, f32[12,448]{1,0:T(8,128)S(1)} %get-tuple-element.120, f32[12,448]{1,0:T(8,128)S(1)} %log_add_fusion), kind=kLoop, calls=%fused_computation | loop fusion | flops 19267584 | bytes 48211968 | tf_op jit(solution)/shard_map/convert_element_type | solution.py:456
  325.3 1.7 multiply_bitcast_fusion
  327.0 1.6 slice.124
  328.9 5.1 bitcast_reduce_fusion
  334.0 6.5 multiply_convert_fusion.3
  340.5 4.7 convolution_convert_fusion.1
  345.3 3.5 convolution_convert_fusion.5
  348.9 2.1 fusion.90
  351.0 1.3 fusion.37
  352.4 4.1 convolution_convert_fusion.3
  356.5 1.8 convolution_convert_fusion.7
  360.2 4.2 convolution_convert_fusion.2
  365.7 174.7 %shard_map.349 = (bf16[2,2,2,384,768]{4,3,2,1,0:T(8,128)(2,1)}, bf16[1,2,2,192,3072]{4,3,2,1,0:T(8,128)(2,1)}, bf16[1,2,2,192,768]{4,3,2,1,0:T(8,128)(2,1)}, bf1...) custom-call(bf16[2,2,2,384,768]{4,3,2,1,0:T(8,128)(2,1)} %bitcast.137, ...), custom_call_target="tpu_custom_call" | custom-call | tf_op jit(solution)/shard_map/pallas_call | solution.py:189
  542.7 6.2 convolution_convert_fusion.4
  548.9 3.1 copy.74
  552.0 10.6 %copy.76 = bf16[448,3,32,32]{2,3,1,0:T(8,128)(2,1)} copy(bf16[448,3,32,32]{0,3,2,1:T(8,128)(2,1)S(1)} %bitcast.125) | data formatting | bytes 5505024 | tf_op jit(solution)/shard_map/reshape | solution.py:497
  562.6 14.3 %fusion.101 = f32[448,48,96]{1,2,0} fusion(bf16[448,32,96]{1,2,0:T(8,128)(2,1)} %bitcast.122, bf16[448,48,32]{1,2,0:T(8,128)(2,1)} %copy.75), kind=kOutput, calls=%fused_computation.200 | convolution fusion | flops 132120576 | bytes 12386304
  576.9 16.0 %fusion.10 = bf16[448,3,48,48]{3,2,1,0:T(8,128)(2,1)} fusion(bf16[448,48,32,1]{1,2,3,0:T(8,128)(2,1)S(1)} %copy-done.3, f32[448,48,3,32]{1,3,2,0:T(8,128)} %bitcast.121), kind=kOutput, calls=%fused_computation.16 | convolution fusion | flops 203341824 | bytes 15826944 | tf_op jit(solution)/shard_map/ncib,njb->ncij/dot_general | solution.py:503
  593.0 18.8 %copy.78 = bf16[448,3,48,48]{0,3,2,1:T(8,128)(2,1)} copy(bf16[448,3,48,48]{3,2,1,0:T(8,128)(2,1)} %fusion.10) | data formatting | bytes 12386304 | tf_op jit(solution)/shard_map/convert_element_type | solution.py:505
  611.8 9.8 %copy.79 = bf16[448,6912]{1,0:T(8,128)(2,1)} copy(bf16[448,6912]{0,1:T(8,128)(2,1)} %bitcast.123) | data formatting | bytes 12386304
  621.6 7.0 %bitcast_convert_fusion.2 = f32[3072,768]{1,0:T(8,128)} fusion(bf16[2,2,2,384,768]{4,3,2,1,0:T(8,128)(2,1)} %get-tuple-element.24), kind=kLoop, calls=%fused_computation.43 | loop fusion | flops 2359296 | bytes 14155776 | tf_op jit(solution)/shard_map/convert_element_type | solution.py:233
  628.5 3.7 bitcast_convert_fusion.3
  632.2 1.7 bitcast_convert_fusion.4
  633.9 5.3 bitcast_convert_fusion.1
  639.9 6.9 %bitcast_convert_fusion = f32[3072,768]{1,0:T(8,128)} fusion(bf16[2,2,2,384,768]{4,3,2,1,0:T(8,128)(2,1)} %get-tuple-element.29), kind=kLoop, calls=%fused_computation.41 | loop fusion | flops 2359296 | bytes 14155776 | tf_op jit(solution)/shard_map/convert_element_type | solution.py:233
  (155 shorter events, 18.1 us)
Async XLA Ops:
  7.2 34.7 %copy-start = (bf16[49,48,32]{0,2,1:T(8,128)(2,1)S(1)}, bf16[49,48,32]{0,2,1:T(8,128)(2,1)}, u32[]{:S(2)}) copy-start(bf16[49,48,32]{0,2,1:T(8,128)(2,1)} %param.25) | copy-start | bytes 451588
  7.2 110.9 %all-gather.6.cloned.1.call-start = ((), (), s32[]{:S(2)}) async-start(), calls=%async_computation | async-start | bytes 5013504 | tf_op jit(solution)/shard_map/all_gather | solution.py:352
  7.9 117.2 %all-gather.8.cloned.1.call-start = ((), (), s32[]{:S(2)}) async-start(), calls=%async_computation.1 | async-start | bytes 3760128 | tf_op jit(solution)/shard_map/all_gather | solution.py:354
  8.7 168.2 %all-gather.10.cloned.1.call-start = ((), (), s32[]{:S(2)}) async-start(), calls=%async_computation.2 | async-start | bytes 1253376 | tf_op jit(solution)/shard_map/all_gather | solution.py:355
  9.4 199.3 %all-gather.12.cloned.1.call-start = ((), (), s32[]{:S(2)}) async-start(), calls=%async_computation.3 | async-start | bytes 5013504 | tf_op jit(solution)/shard_map/all_gather | solution.py:356
  10.0 252.7 %all-gather.14.cloned.1.call-start = ((), (), s32[]{:S(2)}) async-start(), calls=%async_computation.4 | async-start | bytes 5013504 | tf_op jit(solution)/shard_map/all_gather | solution.py:357
  118.1 6.2 copy-start.22
  118.1 6.2 copy-start.31
  124.3 0.9 copy-start.29
  124.3 0.9 copy-start.40
  124.8 4.4 copy-start.4
  124.8 4.4 copy-start.24
  125.1 4.1 copy-start.26
  129.2 2.0 copy-start.16
  132.1 6.5 copy-start.33
  132.1 6.5 copy-start.34
  133.5 8.1 %copy-start.9 = (bf16[448,768]{0,1:T(8,128)(2,1)}, bf16[448,768]{0,1:T(8,128)(2,1)S(1)}, u32[]{:S(2)}) copy-start(bf16[448,768]{0,1:T(8,128)(2,1)S(1)} %copy.72) | copy-start | bytes 2064388
  133.6 19.1 %collective-permute-start.1 = (bf16[448,12,64]{0,2,1:T(8,128)(2,1)S(1)}, bf16[448,12,64]{0,2,1:T(8,128)(2,1)}, u32[]{:S(2)}, u32[]{:S(2)}) collective-permute-start(bf16[448,12,64]{0,2,1:T(8,128)(2,1)S(1)} %bitcast.128), channel_id=1, source_target_pairs={{0,1},{1,0},{2,3},{3,2},{4,5},{5,4},{6,7},{7,6},{8,9},{9,8},{10,11... | collective-permute-start | bytes 2064392 | tf_op jit(solution)/shard_map/ppermute | solution.py:250
  144.1 25.4 %collective-permute-start = (bf16[448,12,64]{0,2,1:T(8,128)(2,1)}, bf16[448,12,64]{0,2,1:T(8,128)(2,1)}, u32[]{:S(2)}, u32[]{:S(2)}) collective-permute-start(bf16[448,12,64]{0,2,1:T(8,128)(2,1)} %bitcast.12), channel_id=1, source_target_pairs={{0,1},{1,0},{2,3},{3,2},{4,5},{5,4},{6,7},{7,6},{8,9},{9,8},{10,11... | collective-permute-start | bytes 2064392 | tf_op jit(solution)/shard_map/ppermute | solution.py:250
  158.5 11.1 %copy-start.2 = (f32[12,448,896]{2,1,0:T(8,128)}, f32[12,448,896]{2,1,0:T(8,128)S(1)}, u32[]{:S(2)}) copy-start(f32[12,448,896]{2,1,0:T(8,128)S(1)} %get-tuple-element.116) | copy-start | bytes 57802756
  163.3 13.7 %copy-start.32 = (f32[768]{0:T(1024)S(1)}, f32[768]{0:T(1024)}, u32[]{:S(2)}) copy-start(f32[768]{0:T(1024)} %param.36) | copy-start | bytes 9220
  176.9 31.9 %copy-start.28 = (f32[768]{0:T(1024)S(1)}, f32[768]{0:T(1024)}, u32[]{:S(2)}) copy-start(f32[768]{0:T(1024)} %param.37) | copy-start | bytes 9220
  176.9 31.9 %copy-start.37 = (f32[3072]{0:T(1024)S(1)}, f32[3072]{0:T(1024)}, u32[]{:S(2)}) copy-start(f32[3072]{0:T(1024)} %param.40) | copy-start | bytes 36868
  176.9 31.9 %copy-start.38 = (f32[768]{0:T(1024)S(1)}, f32[768]{0:T(1024)}, u32[]{:S(2)}) copy-start(f32[768]{0:T(1024)} %param.38) | copy-start | bytes 9220
  272.6 5.1 copy-start.35
  277.7 3.1 copy-start.20
  280.1 2.7 copy-start.17
  281.7 1.1 copy-start.12
  286.6 12.5 %copy-start.11 = (bf16[448,768]{0,1:T(8,128)(2,1)S(1)}, bf16[448,768]{0,1:T(8,128)(2,1)}, u32[]{:S(2)}) copy-start(bf16[448,768]{0,1:T(8,128)(2,1)} %copy.73) | copy-start | bytes 2064388
  295.1 1.5 copy-start.8
  297.8 51.0 %collective-permute-start.3 = (bf16[448,12,64]{0,2,1:T(8,128)(2,1)}, bf16[448,12,64]{0,2,1:T(8,128)(2,1)}, u32[]{:S(2)}, u32[]{:S(2)}) collective-permute-start(bf16[448,12,64]{0,2,1:T(8,128)(2,1)} %slice.123), channel_id=1, source_target_pairs={{0,1},{1,0},{2,3},{3,2},{4,5},{5,4},{6,7},{7,6},{8,9},{9,8},{10,11... | collective-permute-start | bytes 2064392 | tf_op jit(solution)/shard_map/ppermute | solution.py:250
  325.3 3.6 copy-start.10
  327.0 7.0 %copy-start.6 = (f32[896,12,64]{0,2,1:T(8,128)}, f32[896,12,64]{0,2,1:T(8,128)S(1)}, u32[]{:S(2)}) copy-start(f32[896,12,64]{0,2,1:T(8,128)S(1)} %multiply_bitcast_fusion) | copy-start | bytes 8257540
  328.6 5.4 copy-start.39
  328.6 22.4 %collective-permute-start.2 = (bf16[448,12,64]{0,2,1:T(8,128)(2,1)}, bf16[448,12,64]{0,2,1:T(8,128)(2,1)}, u32[]{:S(2)}, u32[]{:S(2)}) collective-permute-start(bf16[448,12,64]{0,2,1:T(8,128)(2,1)} %slice.124), channel_id=1, source_target_pairs={{0,1},{1,0},{2,3},{3,2},{4,5},{5,4},{6,7},{7,6},{8,9},{9,8},{10,11... | collective-permute-start | bytes 2064392 | tf_op jit(solution)/shard_map/ppermute | solution.py:250
  334.0 6.5 copy-start.21
  334.0 6.5 copy-start.42
  345.2 5.8 copy-start.7
  348.9 3.5 copy-start.5
  348.9 3.5 copy-start.19
  348.9 3.5 copy-start.25
  348.9 3.5 copy-start.27
  348.9 3.5 copy-start.30
  348.9 3.5 copy-start.41
  352.4 4.1 copy-start.36
  356.5 2.6 copy-start.13
  358.4 1.9 copy-start.15
  360.2 4.2 copy-start.23
  562.6 14.4 %copy-start.3 = (bf16[448,48,32,1]{1,2,3,0:T(8,128)(2,1)S(1)}, bf16[448,48,32,1]{1,2,3,0:T(8,128)(2,1)}, u32[]{:S(2)}) copy-start(bf16[448,48,32,1]{1,2,3,0:T(8,128)(2,1)} %copy.81) | copy-start | bytes 4128772
  621.5 7.0 %copy-start.14 = (bf16[1,2,2,192,2304]{4,3,2,1,0:T(8,128)(2,1)S(1)}, bf16[1,2,2,192,2304]{4,3,2,1,0:T(8,128)(2,1)}, u32[]{:S(2)}) copy-start(bf16[1,2,2,192,2304]{4,3,2,1,0:T(8,128)(2,1)} %get-tuple-element.26) | copy-start | bytes 10616836
  621.6 12.3 %slice-start = ((s8[4718592]{0:T(1024)(128)(4,1)}), s8[4194304]{0:T(1024)(128)(4,1)S(1)}, s32[]{:S(2)}) async-start(s8[4718592]{0:T(1024)(128)(4,1)} %bitcast.134), calls=%async_computation.5 | async-start | bytes 8388608
  628.5 3.7 copy-start.18
  628.5 5.4 slice-start.1
  639.9 6.9 %copy-start.1 = (bf16[49,48,32]{0,2,1:T(8,128)(2,1)S(1)}, bf16[49,48,32]{0,2,1:T(8,128)(2,1)}, u32[]{:S(2)}) copy-start(bf16[49,48,32]{0,2,1:T(8,128)(2,1)} %param.25) | copy-start | bytes 451588
Sparse Core Ops, SparseCore 0:
  10.3 56.0 all-gather.5
  68.7 45.7 all-gather.7
  116.8 37.4 all-gather.9
  156.5 52.2 all-gather.11
  210.9 51.7 all-gather.13

commit v2 on v1

v2 whole, which is shorter than its diff:
```python
import functools

import jax
import jax.numpy as jnp
import numpy as np
from jax import lax
from jax.experimental import pallas as pl
from jax.experimental.pallas import tpu as pltpu
from jax.sharding import PartitionSpec as P

HEADS = 12
HEAD_DIM = 64
BASE = 32
GRID = 7
PMAX = 48
IMG_SIDE = 240
GTAB = 31


EPS = 1e-06
NEG = -1e30


def from_behind(value, axis, by):
    peers = lax.axis_size(axis)
    return lax.ppermute(value, axis, [(i, (i + by) % peers) for i in range(peers)])


MESH = pl.DeviceIdType.MESH


def place():
    me, y = lax.axis_index("dp"), lax.axis_index("seq")
    core = lax.rem(me, 2)
    x = lax.rem(me // 2, 2)
    z = me // 4
    return me, core, x, y, z


def peers():
    me, core, x, y, z = place()
    sib = (me + 1 - 2 * core, y)
    xn = (me + 2 - 4 * x, y)
    yn = (me, 1 - y)
    zn = [(lax.rem(z + k, 4) * 4 + x * 2 + core, y) for k in (1, 2, 3)]
    return sib, xn, yn, zn


def greet():
    sib, xn, yn, zn = peers()
    barrier = pltpu.get_barrier_semaphore()
    for other in [sib, xn, yn] + zn:
        pl.semaphore_signal(barrier, inc=1, device_id=other, device_id_type=MESH)
    pl.semaphore_wait(barrier, 6)


def add_rows(dst, src, rows, step):
    def one(i, carry):
        at = pl.ds(pl.multiple_of(i * step, step), step)
        dst[at, :] = dst[at, :] + src[at, :]
        return carry

    lax.fori_loop(0, rows // step, one, 0)


class Chunk:
    def __init__(self, array, j, rq, col, h):
        self.array, self.j, self.rq, self.col, self.h = array, j, rq, col, h


def reduce_kernel(chunks, n_in, *refs):
    ins, outs = refs[:n_in], refs[n_in : 2 * n_in]
    rest = list(refs[2 * n_in :])
    n = len(chunks)
    send, recv, loc = rest[-3:]
    bufs = [rest[i * 7 : i * 7 + 7] for i in range(n)]
    me, core, x, y, z = place()
    sib, xn, yn, zn = peers()
    greet()
    started = {}

    def remote(w, number, src, dst, to):
        cp = pltpu.make_async_remote_copy(
            src_ref=src, dst_ref=dst, send_sem=send.at[w, number], recv_sem=recv.at[w, number],
            device_id=to, device_id_type=MESH)
        cp.start()
        started[w, number] = cp

    def stage(w, s):
        c = chunks[w]
        g, out = ins[c.array].at[c.j], outs[c.array].at[c.j]
        own, acc, a1, b1, a2, b2, zz = bufs[w]
        rq, h = c.rq, c.h
        ha, rz = rq // 2, rq // 4
        mine = pl.ds(pl.multiple_of(c.col + core * h, 128), h)
        theirs = pl.ds(pl.multiple_of(c.col + (1 - core) * h, 128), h)
        step = 96 if ha % 96 == 0 else 32
        if s == 0:
            remote(w, 0, g.at[:, :, :, theirs], acc, sib)
            cp = pltpu.make_async_copy(g.at[:, :, :, mine], own, loc.at[w, 0])
            cp.start()
            started[w, "own"] = cp
        if s == 1:
            started[w, "own"].wait()
            started[w, 0].wait_recv()
            for i in range(2):
                for k in range(2):
                    add_rows(acc.at[i, k], own.at[i, k], rq, step)
            remote(w, 1, acc.at[1 - x, :, pl.ds(0, ha), :], a1, xn)
            remote(w, 2, acc.at[:, 1 - y, pl.ds(ha, ha), :], b1, yn)
        if s == 2:
            started[w, 1].wait_recv()
            started[w, 2].wait_recv()
            add_rows(acc.at[x, 1 - y, pl.ds(0, ha)], a1.at[1 - y], ha, step)
            remote(w, 3, acc.at[x, 1 - y, pl.ds(0, ha), :], a2, yn)
            add_rows(acc.at[1 - x, y, pl.ds(ha, ha)], b1.at[1 - x], ha, step)
            remote(w, 4, acc.at[1 - x, y, pl.ds(ha, ha), :], b2, xn)
            add_rows(acc.at[x, y, pl.ds(0, ha)], a1.at[y], ha, step)
            add_rows(acc.at[x, y, pl.ds(ha, ha)], b1.at[x], ha, step)
        if s == 3:
            started[w, 3].wait_recv()
            started[w, 4].wait_recv()
            add_rows(acc.at[x, y, pl.ds(0, ha)], a2, ha, step)
            add_rows(acc.at[x, y, pl.ds(ha, ha)], b2, ha, step)
            for k in (1, 2, 3):
                rows = pl.ds(pl.multiple_of(lax.rem(z + k, 4) * rz, 16), rz)
                remote(w, 4 + k, acc.at[x, y, rows, :], zz.at[k - 1], zn[k - 1])
        if s == 4:
            for k in (1, 2, 3):
                started[w, 4 + k].wait_recv()

            def total(i, carry):
                at = pl.ds(pl.multiple_of(i * 16, 16), 16)
                here = pl.ds(pl.multiple_of(z * rz + i * 16, 16), 16)
                f = lambda v: v.astype(jnp.float32)
                both = f(acc[x, y, here, :]) + f(zz[0, at, :])
                both = both + f(zz[1, at, :]) + f(zz[2, at, :])
                zz[3, at, :] = both.astype(jnp.bfloat16)
                return carry

            lax.fori_loop(0, rz // 16, total, 0)
            rows = pl.ds(pl.multiple_of(z * rz, 16), rz)
            for k in (1, 2, 3):
                remote(w, 7 + k, zz.at[3], out.at[x, y, rows, mine], zn[k - 1])
            cp = pltpu.make_async_copy(zz.at[3], out.at[x, y, rows, mine], loc.at[w, 1])
            cp.start()
            started[w, "fin"] = cp
        if s == 5:
            started[w, "fin"].wait()
            for k in (1, 2, 3):
                started[w, 7 + k].wait_recv()
            part = out.at[x, y, pl.ds(0, ha), mine]
            remote(w, 11, part, part, yn)
            part = out.at[x, y, pl.ds(ha, ha), mine]
            remote(w, 12, part, part, xn)
        if s == 6:
            started[w, 11].wait_recv()
            started[w, 12].wait_recv()
            part = out.at[x, :, pl.ds(0, ha), mine]
            remote(w, 13, part, part, xn)
            part = out.at[:, y, pl.ds(ha, ha), mine]
            remote(w, 14, part, part, yn)
        if s == 7:
            started[w, 13].wait_recv()
            started[w, 14].wait_recv()
            part = out.at[:, :, :, mine]
            remote(w, 15, part, part, sib)
        if s == 8:
            started[w, 15].wait_recv()

    for tick in range(n + 8):
        for w in range(n):
            if 0 <= tick - w <= 8:
                stage(w, tick - w)
    for w in range(n):
        for number in range(16):
            started[w, number].wait_send()


def all_sum(arrays, chunks):
    scratch = []
    for c in chunks:
        ha, rz = c.rq // 2, c.rq // 4
        scratch += [
            pltpu.VMEM((2, 2, c.rq, c.h), jnp.bfloat16),
            pltpu.VMEM((2, 2, c.rq, c.h), jnp.bfloat16),
            pltpu.VMEM((2, ha, c.h), jnp.bfloat16),
            pltpu.VMEM((2, ha, c.h), jnp.bfloat16),
            pltpu.VMEM((ha, c.h), jnp.bfloat16),
            pltpu.VMEM((ha, c.h), jnp.bfloat16),
            pltpu.VMEM((4, rz, c.h), jnp.bfloat16),
        ]
    n = len(chunks)
    scratch += [
        pltpu.SemaphoreType.DMA((n, 16)),
        pltpu.SemaphoreType.DMA((n, 16)),
        pltpu.SemaphoreType.DMA((n, 2)),
    ]
    return pl.pallas_call(
        functools.partial(reduce_kernel, chunks, len(arrays)),
        out_shape=[jax.ShapeDtypeStruct(a.shape, a.dtype) for a in arrays],
        in_specs=[pl.BlockSpec(memory_space=pl.ANY)] * len(arrays),
        out_specs=[pl.BlockSpec(memory_space=pl.ANY)] * len(arrays),
        scratch_shapes=scratch,
        compiler_params=pltpu.CompilerParams(
            collective_id=1, has_side_effects=True, vmem_limit_bytes=60 * 2**20),
    )(*arrays)

CHUNKS = [
    Chunk(0, 0, 384, 0, 384),
    Chunk(0, 1, 384, 0, 384),
    Chunk(1, 0, 192, 0, 768),
    Chunk(1, 0, 192, 1536, 768),
    Chunk(2, 0, 192, 0, 384),
    Chunk(3, 0, 192, 0, 640),
    Chunk(3, 0, 192, 1280, 512),
    Chunk(4, 0, 384, 0, 384),
    Chunk(4, 1, 384, 0, 384),
    Chunk(5, 0, 64, 0, 384),
]


def linked():
    return lax.axis_size("dp") == 16 and lax.axis_size("seq") == 2


def summed_over_devices(members):
    if not linked():
        return [lax.psum(member, ("dp", "seq")) for member in members]
    arrays = []
    for member, parts in zip(members, (2, 1, 1, 1, 2, 1)):
        quarter = member.shape[0] // (4 * parts)
        arrays.append(member.reshape(parts, 2, 2, quarter, member.shape[1]))
    return [d.reshape(m.shape) for d, m in zip(all_sum(arrays, CHUNKS), members)]


F32, BF = jnp.float32, jnp.bfloat16
SLOTS, BIG, SMALL = 448, 256, 64
BLOCKS = ((0, 256), (256, 64), (320, 64), (384, 64))
VMEM_CAP = 60 * 2**20


def nn(a, b):
    return lax.dot_general(a, b, (((1,), (0,)), ((), ())), preferred_element_type=F32)


def nt(a, b):
    return lax.dot_general(a, b, (((1,), (1,)), ((), ())), preferred_element_type=F32)


def tn(a, b):
    return lax.dot_general(a, b, (((0,), (0,)), ((), ())), preferred_element_type=F32)


def tile(i, size):
    return pl.ds(pl.multiple_of(i * size, size), size)


def loop(count, body):
    def one(i, carry):
        body(i)
        return carry

    lax.fori_loop(0, count, one, 0)


class Refs:
    pass


def picks(r):
    slots = lax.broadcasted_iota(jnp.int32, (SLOTS, SLOTS), 1)
    r.pick[...] = jnp.where(r.src_col[...] == slots, 1.0, 0.0).astype(BF)


def picks_back(r):
    slots = lax.broadcasted_iota(jnp.int32, (SLOTS, SLOTS), 0)
    r.pick_t[...] = jnp.where(r.src_row[...] == slots, 1.0, 0.0).astype(BF)


def resize_factors(r):
    def one(c):
        table = r.tables[c]
        first = nn(r.e1[...], table).astype(BF)
        r.w1[c] = nn(first, r.e2[...]).astype(BF) * r.m1[...]
        second = nn(r.e3[...], table).astype(BF)
        r.w2[c] = nn(second, r.e4[...]).astype(BF) * r.m2[...]

    loop(4, one)


def position_weights(r):
    lanes = lax.broadcasted_iota(jnp.int32, (SLOTS, 128), 1)
    high = lax.Precision.HIGHEST
    row = jnp.where(r.row_at[...] == lanes, 1.0, 0.0)
    col = jnp.where(r.col_at[...] == lanes, 1.0, 0.0)
    row = jnp.dot(row, r.row_table[...], precision=high, preferred_element_type=F32)
    col = jnp.dot(col, r.col_table[...], precision=high, preferred_element_type=F32)
    r.posw[...] = (row * col).astype(BF)


def resize_channel(r, ch):
    base = ch * 2304
    big = nn(r.pick[0:BIG, :], r.pixels[:, base : base + 768]).astype(BF)
    for g in range(2):
        half = nn(big[:, g * 384 : g * 384 + 384], r.w1[0]).astype(BF)
        for bh in range(2):
            r.half_big[ch * 2 + bh, :, g * 128 : g * 128 + 128] = half[:, bh * 128 : bh * 128 + 128]
    for third in range(3):
        lo = third * 768
        r.rest[:, lo : lo + 768] = nn(
            r.pick[BIG:SLOTS, :], r.pixels[:, base + lo : base + lo + 768]
        ).astype(BF)
    for m in range(3):
        rows = slice(m * 64, m * 64 + 64)
        joined = jnp.concatenate([r.rest[rows, g * 384 : g * 384 + 384] for g in range(6)], axis=0)
        half = nn(joined, r.w1[m + 1]).astype(BF)
        for g in range(6):
            for bh in range(2):
                r.half_small[ch * 2 + bh, rows, g * 128 : g * 128 + 128] = half[
                    g * 64 : g * 64 + 64, bh * 128 : bh * 128 + 128
                ]


def resize_rows(r):
    for n in range(6):
        r.patches[0:BIG, n * 512 : n * 512 + 512] = nn(r.half_big[n], r.w2[0, 0:256, :]).astype(BF)
    for m in range(3):
        joined = jnp.concatenate([r.half_small[n, m * 64 : m * 64 + 64, :] for n in range(6)], axis=0)
        done = nn(joined, r.w2[m + 1]).astype(BF)
        at = BIG + m * 64
        for n in range(6):
            r.patches[at : at + 64, n * 512 : n * 512 + 512] = done[n * 64 : n * 64 + 64, :]


def embed_tile(r, n):
    at = tile(n, 256)
    r.embed[:, at] = (
        nt(r.patches[...], r.base_t[at, 0:3072]) + nt(r.posw[...], r.base_t[at, 3072:3200]) + r.embed_bias[:, at]
    )


def norm_rows(values):
    centred = values - jnp.mean(values, axis=-1, keepdims=True)
    inverse = lax.rsqrt(jnp.mean(centred * centred, axis=-1, keepdims=True) + EPS)
    return centred * inverse, inverse


def norm_forward(source, gain, bias, out):
    def one(i):
        at = tile(i, 64)
        normed, _ = norm_rows(source[at, :])
        out[at, :] = (normed * gain[...] + bias[...]).astype(BF)

    loop(7, one)


def keys_values(r, side, hidden):
    for n in range(3):
        at = pl.ds(n * 256, 256)
        r.keys[side, :, at] = nt(hidden[...], r.qkv_t[pl.ds(768 + n * 256, 256), :]).astype(BF)
        r.values[side, :, at] = (
            nt(hidden[...], r.qkv_t[pl.ds(1536 + n * 256, 256), :]) + r.value_bias[:, at]
        ).astype(BF)


def queries(r):
    for n in range(3):
        at = pl.ds(n * 256, 256)
        whole = (nt(r.hidden1[...], r.qkv_t[at, :]) + r.query_bias[:, at]).astype(BF)
        r.query[:, at] = whole * jnp.asarray(HEAD_DIM ** (-0.5), BF)


def both_sides(array, start, count, at):
    return jnp.concatenate(
        [array[0, pl.ds(start, count), at], array[1, pl.ds(start, count), at]], axis=0
    )


def attention_forward(r):
    def one(pair):
        at = tile(pair, 128)
        for index, (start, count) in enumerate(BLOCKS):
            rows = pl.ds(start, count)
            query = r.query[rows, at]
            keys = both_sides(r.keys, start, count, at)
            values = both_sides(r.values, start, count, at)
            first = lax.broadcasted_iota(jnp.int32, (count, 128), 1) < HEAD_DIM
            outs = []
            for head in range(2):
                mine = first if head == 0 else jnp.logical_not(first)
                only = jnp.where(mine, query, jnp.zeros_like(query))
                scores = nt(only, keys)
                if index == 0:
                    scores = scores + r.big_row[...]
                else:
                    scores = scores + r.small_row[index - 1 : index, :]
                top = jnp.max(scores, axis=-1, keepdims=True)
                exponent = jnp.exp(scores - top)
                total = jnp.sum(exponent, axis=-1, keepdims=True)
                probs = (exponent * (1.0 / total)).astype(BF)
                outs.append(nn(probs, values))
            r.attended[rows, at] = jnp.where(first, outs[0], outs[1]).astype(BF)

    loop(6, one)


def project(r):
    for n in range(3):
        at = pl.ds(n * 256, 256)
        r.middle[:, at] = r.embed[:, at] + nt(r.attended[...], r.proj_t[at, :]) + r.proj_bias[:, at]


def feed_in(r, n):
    at = tile(n, 256)
    r.pre[...] = nt(r.hidden2[...], r.fc1_t[at, :]) + r.fc1_bias[:, at]

    def one(i):
        rows = tile(i, 32)
        value = r.pre[rows, :]
        chance = 0.5 + 0.5 * lax.erf(value * (0.5**0.5))
        density = jnp.exp(value * value * -0.5) * 0.3989422804014327
        r.act[rows, at] = (value * chance).astype(BF)
        r.slope[rows, at] = (chance + value * density).astype(BF)

    loop(14, one)


def feed_out(r):
    for n in range(3):
        at = pl.ds(n * 256, 256)
        whole = r.middle[:, at] + (nt(r.act[...], r.fc2_t[at, :]) + r.fc2_bias[:, at])
        r.block_out[:, at] = nn(r.pick_t[...], whole.astype(BF)).astype(BF)


def column_sum(array):
    ones = jnp.ones((16, SLOTS), BF)
    return nn(ones, array)[0:1, :]


def cotangent_in(r):
    for n in range(3):
        at = pl.ds(n * 256, 256)
        r.grad_final[:, at] = nn(r.pick[...], r.cotangent[:, at]).astype(BF)
    r.rows[12:13, :] = column_sum(r.grad_final[...])


def grad_fc2_tile(r, n, out):
    at = tile(n, 256)
    out[...] = tn(r.act[:, at], r.grad_final[...]).astype(BF)


def grad_pre_tile(r, n):
    at = tile(n, 256)
    back = nn(r.grad_final[...], r.fc2_t[:, at])
    r.grad_pre[:, at] = (back * r.slope[:, at].astype(F32)).astype(BF)


def grad_hidden2(r):
    for n in range(3):
        at = pl.ds(n * 256, 256)
        r.grad_norm[:, at] = nn(r.grad_pre[...], r.fc1_t[:, at]).astype(BF)


def norm_backward(r, source, gain, plus, gain_row, bias_row, store):
    r.rows[gain_row : gain_row + 1, :] = jnp.zeros((1, 768), F32)
    r.rows[bias_row : bias_row + 1, :] = jnp.zeros((1, 768), F32)

    def one(i):
        at = tile(i, 64)
        normed, inverse = norm_rows(source[at, :])
        grad = r.grad_norm[at, :].astype(F32)
        r.rows[gain_row : gain_row + 1, :] += jnp.sum(grad * normed, axis=0, keepdims=True)
        r.rows[bias_row : bias_row + 1, :] += jnp.sum(grad, axis=0, keepdims=True)
        e = grad * gain[...]
        back = inverse * (
            e
            - jnp.mean(e, axis=-1, keepdims=True)
            - normed * jnp.mean(e * normed, axis=-1, keepdims=True)
        )
        store(at, plus[at, :].astype(F32) + back)

    loop(7, one)


def middle_backward(r):
    def store(at, value):
        r.grad_middle[at, :] = value
        r.grad_branch[at, :] = value.astype(BF)

    norm_backward(r, r.middle, r.norm2_gain, r.grad_final, 6, 7, store)
    r.rows[5:6, :] = column_sum(r.grad_branch[...])


def attended_backward(r):
    for n in range(3):
        at = pl.ds(n * 256, 256)
        r.grad_attended[:, at] = nn(r.grad_branch[...], r.proj_t[:, at]).astype(BF)


def attention_backward(r):
    def one(pair):
        at = tile(pair, 128)
        for index, (start, count) in enumerate(BLOCKS):
            rows = pl.ds(start, count)
            query = r.query[rows, at]
            grad = r.grad_attended[rows, at]
            keys = both_sides(r.keys, start, count, at)
            values = both_sides(r.values, start, count, at)
            first = lax.broadcasted_iota(jnp.int32, (count, 128), 1) < HEAD_DIM
            grad_query, grad_keys, grad_values = [], [], []
            for head in range(2):
                mine = first if head == 0 else jnp.logical_not(first)
                only = jnp.where(mine, query, jnp.zeros_like(query))
                grad_only = jnp.where(mine, grad, jnp.zeros_like(grad))
                scores = nt(keys, only)
                if index == 0:
                    scores = scores + r.big_col[...]
                else:
                    scores = scores + r.small_col[:, index - 1 : index]
                top = jnp.max(scores, axis=0, keepdims=True)
                exponent = jnp.exp(scores - top)
                total = jnp.sum(exponent, axis=0, keepdims=True)
                probs = exponent * (1.0 / total)
                grad_probs = nt(values, grad_only)
                share = jnp.sum(probs * grad_probs, axis=0, keepdims=True)
                grad_scores = (probs * (grad_probs - share)).astype(BF)
                grad_query.append(tn(grad_scores, keys))
                grad_keys.append(nn(grad_scores, only))
                grad_values.append(nn(probs.astype(BF), grad_only))
            both = jnp.where(first, grad_query[0], grad_query[1]) * HEAD_DIM ** (-0.5)
            r.grad_query[rows, at] = both.astype(BF)
            both = (grad_keys[0] + grad_keys[1]).astype(BF)
            r.grad_keys[0, rows, at] = both[0:count]
            r.grad_keys[1, rows, at] = both[count:]
            both = (grad_values[0] + grad_values[1]).astype(BF)
            r.grad_values[0, rows, at] = both[0:count]
            r.grad_values[1, rows, at] = both[count:]

    loop(6, one)


def far_back(r):
    for n in range(3):
        at = pl.ds(n * 256, 256)
        r.far_grad[:, at] = (
            nn(r.grad_keys[1], r.qkv_t[pl.ds(768, 768), at])
            + nn(r.grad_values[1], r.qkv_t[pl.ds(1536, 768), at])
        ).astype(BF)


def bias_rows(r):
    r.rows[3:4, :] = column_sum(r.grad_query[...])
    r.rows[4:5, :] = column_sum(r.grad_values[0]) + column_sum(r.grad_values[1])
    for n in range(4):
        r.rows[8 + n : 9 + n, :] = column_sum(r.grad_pre[:, n * 768 : n * 768 + 768])


def grad_qkv(r, out):
    r.hidden_t[...] = r.hidden1[...].T
    r.far_t[...] = r.hidden_far[...].T
    for n in range(3):
        at = pl.ds(n * 256, 256)
        out(n)[...] = nn(r.hidden_t[...], r.grad_query[:, at]).astype(BF)
    for k, array in ((1, r.grad_keys), (2, r.grad_values)):
        for n in range(3):
            at = pl.ds(n * 256, 256)
            out(3 * k + n)[...] = (
                nn(r.hidden_t[...], array[0, :, at]) + nn(r.far_t[...], array[1, :, at])
            ).astype(BF)


def hidden1_backward(r):
    for n in range(3):
        at = pl.ds(n * 256, 256)
        r.grad_norm[:, at] = (
            nn(r.grad_query[...], r.qkv_t[pl.ds(0, 768), at])
            + nn(r.grad_keys[0], r.qkv_t[pl.ds(768, 768), at])
            + nn(r.grad_values[0], r.qkv_t[pl.ds(1536, 768), at])
            + r.far_in[:, at].astype(F32)
        ).astype(BF)


def embed_backward(r):
    def store(at, value):
        r.grad_embed[at, :] = value.astype(BF)

    norm_backward(r, r.embed, r.norm1_gain, r.grad_middle, 1, 2, store)
    r.rows[0:1, :] = column_sum(r.grad_embed[...])


def grad_base_tile(r, n, out):
    at = tile(n, 256)
    out[...] = tn(r.patches[:, at], r.grad_embed[...]).astype(BF)


def small_sums(r):
    r.small[0:128, :] = tn(r.posw[...], r.grad_embed[...]).astype(BF)
    r.small[128:144, :] = r.rows[...].astype(BF)
    r.small[144:256, :] = jnp.zeros((112, 768), BF)


def patches_backward(r, n):
    at = tile(n, 512)
    r.grad_patches[:, at] = nn(r.grad_embed[...], r.base_t[:, at]).astype(BF)


def resize_backward(r):
    for n in range(6):
        r.half_big[n] = nt(r.grad_patches[0:BIG, n * 512 : n * 512 + 512], r.w2[0, 0:256, :]).astype(BF)
    for m in range(3):
        at = BIG + m * 64
        joined = jnp.concatenate(
            [r.grad_patches[at : at + 64, n * 512 : n * 512 + 512] for n in range(6)], axis=0
        )
        done = nt(joined, r.w2[m + 1]).astype(BF)
        for n in range(6):
            r.half_small[n, m * 64 : m * 64 + 64, :] = done[n * 64 : n * 64 + 64, :]
    for ch in range(3):
        base = ch * 2304
        big = []
        for g in range(2):
            cols = slice(g * 128, g * 128 + 128)
            half = jnp.concatenate([r.half_big[ch * 2, :, cols], r.half_big[ch * 2 + 1, :, cols]], axis=1)
            big.append(nt(half, r.w1[0]).astype(BF))
        for m in range(3):
            rows = slice(m * 64, m * 64 + 64)
            joined = jnp.concatenate(
                [
                    jnp.concatenate(
                        [r.half_small[ch * 2 + bh, rows, g * 128 : g * 128 + 128] for bh in range(2)], axis=1
                    )
                    for g in range(6)
                ],
                axis=0,
            )
            done = nt(joined, r.w1[m + 1]).astype(BF)
            for g in range(6):
                r.rest[rows, g * 384 : g * 384 + 384] = done[g * 64 : g * 64 + 64, :]
        for g in range(2):
            lo = g * 384
            r.pixel_grad[:, base + lo : base + lo + 384] = (
                nn(r.pick_t[:, 0:BIG], big[g]) + nn(r.pick_t[:, BIG:SLOTS], r.rest[:, lo : lo + 384])
            ).astype(BF)
        for g in range(2):
            lo = 768 + g * 768
            r.pixel_grad[:, base + lo : base + lo + 768] = nn(
                r.pick_t[:, BIG:SLOTS], r.rest[:, lo : lo + 768]
            ).astype(BF)


class Gather:
    def __init__(self, shards, wholes, send, recv, local):
        self.shards, self.wholes = shards, wholes
        self.send, self.recv, self.local = send, recv, local
        self.me, self.core, self.x, self.y, self.z = place()
        self.sib, self.xn, self.yn, self.zn = peers()
        self.started, self.used = {}, {}

    def block(self, w, z, x, half):
        rows, cols = self.shards[w].shape
        at = (z * 4 + x * 2 + self.core) * rows
        at = pl.ds(pl.multiple_of(at, 16), rows)
        if half is None:
            return self.wholes[w].at[at, :]
        return self.wholes[w].at[at, pl.ds(pl.multiple_of(half * (cols // 2), 128), cols // 2)]

    def remote(self, w, label, ref, to, src=None):
        number = self.used.get(w, 0)
        self.used[w] = number + 1
        cp = pltpu.make_async_remote_copy(
            src_ref=ref if src is None else src, dst_ref=ref, send_sem=self.send.at[w, number],
            recv_sem=self.recv.at[w, number], device_id=to, device_id_type=MESH)
        cp.start()
        self.started[w, label] = cp

    def arrived(self, w, *labels):
        for label in labels:
            self.started[w, label].wait_recv()

    def stage(self, w, s):
        x, y, z = self.x, self.y, self.z
        far = [lax.rem(z + 4 - k, 4) for k in (1, 2, 3)]
        if s == 0:
            cp = pltpu.make_async_copy(self.shards[w], self.block(w, z, x, None), self.local.at[w])
            cp.start()
            self.started[w, "own"] = cp
            cols = self.shards[w].shape[1] // 2
            half = self.shards[w].at[:, pl.ds(pl.multiple_of(y * cols, 128), cols)]
            for k in (1, 2, 3):
                self.remote(w, ("z", k), self.block(w, z, x, y), self.zn[k - 1], half)
            self.remote(w, "x own", self.block(w, z, x, None), self.xn, self.shards[w])
            self.remote(w, "own", self.block(w, z, x, None), self.sib, self.shards[w])
            self.started[w, "sib own"] = self.started[w, "own"]
            self.started[w, "own"] = cp
        if s == 1:
            for k in (1, 2, 3):
                self.arrived(w, ("z", k))
                got = self.block(w, far[k - 1], x, y)
                self.remote(w, ("x", k), got, self.xn)
                self.remote(w, ("y", k), got, self.yn)
                self.remote(w, ("sib z", k), got, self.sib)
            self.arrived(w, "x own")
            self.remote(w, "sib x own", self.block(w, z, 1 - x, None), self.sib)
        if s == 2:
            for k in (1, 2, 3):
                self.arrived(w, ("x", k))
                got = self.block(w, far[k - 1], 1 - x, y)
                if k < 3:
                    self.remote(w, ("diag", k), got, self.yn)
                self.remote(w, ("sib x", k), got, self.sib)
                self.arrived(w, ("y", k))
                got = self.block(w, far[k - 1], x, 1 - y)
                if k == 3:
                    self.remote(w, ("diag", k), got, self.xn)
                self.remote(w, ("sib y", k), got, self.sib)
        if s == 3:
            for k in (1, 2, 3):
                self.arrived(w, ("diag", k))
                self.remote(w, ("sib diag", k), self.block(w, far[k - 1], 1 - x, 1 - y), self.sib)
        if s == 4:
            self.started[w, "own"].wait()
            self.arrived(w, "sib own", "sib x own")
            for k in (1, 2, 3):
                self.arrived(w, ("sib z", k), ("sib x", k), ("sib y", k), ("sib diag", k))

    def finish(self):
        for (w, label), cp in self.started.items():
            if label != "own":
                cp.wait_send()


GATHER_COPIES = 27


def line_up(n, stages, stage):
    for tick in range(n + stages - 1):
        for w in reversed(range(n)):
            if 0 <= tick - w < stages:
                stage(w, tick - w)
        yield tick


def call_linked(name, collective, body, near, far, outputs, scratch, semaphores):
    names = list(near) + list(far) + [k + "_out" for k in outputs]
    buffers = {k: pltpu.VMEM(s, d) for k, (s, d, kept) in outputs.items() if kept}
    buffers.update({k: pltpu.VMEM(s, d) for k, (s, d) in scratch.items()})
    buffers.update(semaphores)
    names += list(buffers)

    def kernel(*refs):
        r = Refs()
        for label, ref in zip(names, refs):
            setattr(r, label, ref)
        body(r)

    vmem, left = pl.BlockSpec(memory_space=pltpu.VMEM), pl.BlockSpec(memory_space=pl.ANY)
    done = pl.pallas_call(
        kernel,
        out_shape=[jax.ShapeDtypeStruct(s, d) for s, d, _ in outputs.values()],
        in_specs=[vmem] * len(near) + [left] * len(far),
        out_specs=[left] * len(outputs),
        scratch_shapes=list(buffers.values()),
        compiler_params=pltpu.CompilerParams(
            collective_id=collective, has_side_effects=True, vmem_limit_bytes=VMEM_CAP),
        name=name,
    )(*near.values(), *far.values())
    return dict(zip(outputs, done))


class Local:
    def __init__(self, sems):
        self.sems, self.count, self.open = sems, 0, {}

    def start(self, label, src, dst):
        cp = pltpu.make_async_copy(src, dst, self.sems.at[self.count])
        self.count += 1
        cp.start()
        self.open[label] = cp

    def wait(self, *labels):
        for label in labels:
            self.open.pop(label).wait()

    def wait_all(self):
        self.wait(*list(self.open))


WEIGHTS = ("base_t", "qkv_t", "proj_t", "fc1_t", "fc2_t")


def forward_kernel(r):
    local = Local(r.local)
    for ch in range(3):
        at = pl.ds(ch * 2304, 2304)
        local.start(("pixels", ch), r.pixels_in.at[:, at], r.pixels.at[:, at])
    greet()
    ga = Gather([getattr(r, k + "_shard") for k in WEIGHTS], [getattr(r, k) for k in WEIGHTS], r.send, r.recv, r.own)
    me, core, x, y, z = place()
    sib, xn, yn, zn = peers()

    def keep(*labels):
        for label in labels:
            local.start(label, getattr(r, label), getattr(r, label + "_out"))

    def ready(w):
        keep(WEIGHTS[w])

    ticks = line_up(5, 5, ga.stage)
    next(ticks)
    picks(r)
    picks_back(r)
    resize_factors(r)
    keep("w1", "w2")
    next(ticks)
    position_weights(r)
    keep("posw")
    for ch in range(3):
        local.wait(("pixels", ch))
        resize_channel(r, ch)
        if ch == 1:
            next(ticks)
    next(ticks)
    resize_rows(r)
    keep("patches")
    next(ticks)
    ready(0)
    for n in range(3):
        embed_tile(r, n)
    keep("embed")
    norm_forward(r.embed, r.norm1_gain, r.norm1_bias, r.hidden1)
    keep("hidden1")
    swap = pltpu.make_async_remote_copy(
        src_ref=r.hidden1, dst_ref=r.hidden_far, send_sem=r.swap.at[0], recv_sem=r.swap.at[1], device_id=yn,
        device_id_type=MESH)
    swap.start()
    next(ticks)
    ready(1)
    queries(r)
    keep("query")
    keys_values(r, 0, r.hidden1)
    next(ticks)
    ready(2)
    swap.wait_recv()
    keep("hidden_far")
    keys_values(r, 1, r.hidden_far)
    keep("keys", "values")
    attention_forward(r)
    keep("attended")
    project(r)
    keep("middle")
    norm_forward(r.middle, r.norm2_gain, r.norm2_bias, r.hidden2)
    keep("hidden2")
    next(ticks)
    ready(3)
    loop(12, lambda n: feed_in(r, n))
    keep("act", "slope")
    for _ in ticks:
        pass
    ready(4)
    feed_out(r)
    keep("block_out")
    swap.wait_send()
    ga.finish()
    local.wait_all()


def forward_linked(plan, vectors, pixels, shards):
    full, wide, pair = ((SLOTS, 768), BF), ((SLOTS, 3072), BF), ((2, SLOTS, 768), BF)
    exact, square = ((SLOTS, 768), F32), ((SLOTS, SLOTS), BF)
    near = dict(
        **constants(),
        **{k: plan[k] for k in (
            "src_col", "src_row", "tables", "row_at", "col_at", "row_table", "col_table", "big_row", "small_row")},
        **vectors,
    )
    far = dict(pixels_in=pixels, **{k + "_shard": s for k, s in zip(WEIGHTS, shards)})
    outputs = dict(
        block_out=full, patches=wide, posw=((SLOTS, 128), BF), embed=exact, hidden1=full, hidden_far=full, query=full,
        keys=pair, values=pair, attended=full, middle=exact, hidden2=full, act=wide, slope=wide,
        w1=((4, 384, 256), BF), w2=((4, 768, 512), BF),
        **{k: ((16 * s.shape[0], s.shape[1]), BF) for k, s in zip(WEIGHTS, shards)},
    )
    scratch = dict(
        pixels=((SLOTS, 6912), BF), pick=square, pick_t=square, half_big=((6, BIG, 256), BF),
        half_small=((6, 192, 768), BF), rest=((192, 2304), BF), pre=((SLOTS, 256), F32),
    )
    dma = pltpu.SemaphoreType.DMA
    semaphores = dict(
        send=dma((5, GATHER_COPIES)), recv=dma((5, GATHER_COPIES)), own=dma((5,)), swap=dma((2,)),
        local=dma((3 + len(outputs),)),
    )
    return call_linked(
        "forward", 2, forward_kernel, near, far, {k: (s, d, True) for k, (s, d) in outputs.items()}, scratch,
        semaphores)


def back_chunk(w):
    pass


class Backward:
    def __init__(self, stage, stages=9):
        self.stage, self.stages, self.open = stage, stages, []

    def add(self, w):
        self.open.append([w, 0])

    def tick(self):
        for item in reversed(self.open):
            self.stage(item[0], item[1])
            item[1] += 1
        self.open = [item for item in self.open if item[1] < self.stages]


def shards_of(base_kernel, pos_grid, qkv_weight, proj_weight, fc1_weight, fc2_weight):
    across = base_kernel.shape[1]
    base = base_kernel.reshape(3, BASE, 2, 16, across).transpose(0, 2, 1, 3, 4).reshape(3 * BASE * BASE, across)
    base = jnp.concatenate([base, jnp.pad(pos_grid, ((0, 256 - GRID * GRID), (0, 0)))], axis=0)
    return [member.T for member in (base, qkv_weight, proj_weight, fc1_weight, fc2_weight)]


def whole(name, body, inputs, outputs, scratch):
    names = list(inputs) + list(outputs) + list(scratch)

    def kernel(*refs):
        r = Refs()
        for label, ref in zip(names, refs):
            setattr(r, label, ref)
        body(r)

    vmem = pl.BlockSpec(memory_space=pltpu.VMEM)
    done = pl.pallas_call(
        kernel,
        out_shape=[jax.ShapeDtypeStruct(s, d) for s, d in outputs.values()],
        in_specs=[vmem] * len(inputs),
        out_specs=[vmem] * len(outputs),
        scratch_shapes=[pltpu.VMEM(s, d) for s, d in scratch.values()],
        compiler_params=pltpu.CompilerParams(vmem_limit_bytes=VMEM_CAP),
        name=name,
    )(*inputs.values())
    return dict(zip(outputs, done))


def selection(rows, cols, row_of, col_of):
    left = row_of(np.arange(rows))[:, None]
    right = col_of(np.arange(cols))[None, :]
    return jnp.asarray((left == right).astype(np.float32), BF)


def constants():
    return dict(
        e1=selection(384, 48, lambda t: t % 48, lambda t: t),
        e2=selection(32, 256, lambda t: t, lambda t: t // 8),
        m1=selection(384, 256, lambda t: t // 48, lambda t: t % 8),
        e3=selection(768, 48, lambda t: t // 128 * 8 + t % 8, lambda t: t),
        e4=selection(32, 512, lambda t: t, lambda t: t // 16),
        m2=selection(768, 512, lambda t: t // 8 % 16, lambda t: t % 16),
    )


def class_plan(patch_size, rows_first, pos_resize, kernel_resize, side):
    four = jnp.arange(4, dtype=jnp.int32)
    big = jnp.argmin(patch_size).astype(jnp.int32)
    order = jnp.where(four == 0, big, jnp.where(four - 1 < big, four - 1, four))
    chosen = (order[:, None] == four[None, :]).astype(jnp.int32)
    pick = lambda v: jnp.sum(chosen * v[None, :], axis=1)
    grid = IMG_SIDE // patch_size
    counts, firsts = [], []
    for s in (side, 1 - side):
        filled = jnp.where(s == 0, rows_first, grid - rows_first) * grid
        before = jnp.sum(jnp.where(four[None, :] < four[:, None], filled[None, :], 0), axis=1)
        counts.append(pick(filled))
        firsts.append(pick(before))
    patch, grid = pick(patch_size), pick(grid)
    offset = pick(jnp.where(side == 0, 0, rows_first))
    row = np.arange(SLOTS)
    kind = np.where(row < BIG, 0, 1 + (row - BIG) // SMALL)
    within = jnp.asarray(np.where(row < BIG, row, (row - BIG) % SMALL), jnp.int32)
    member = jnp.asarray(kind[:, None] == np.arange(4)[None, :], jnp.int32)
    spread = lambda v: jnp.sum(member * v[None, :], axis=1)
    live = within < spread(counts[0])
    source = jnp.where(live, spread(firsts[0]) + within, -1)
    side_length = spread(grid)
    start = jnp.asarray(kind * GTAB, jnp.int32)
    row_at = jnp.where(live, start + within // side_length + spread(offset), -1)
    col_at = jnp.where(live, start + within % side_length, -1)
    low = lambda ok: jnp.where(ok, 0.0, NEG).astype(F32)
    near, far = low(live), low(within < spread(counts[1]))
    small_row = jnp.concatenate([near[BIG:].reshape(3, SMALL), far[BIG:].reshape(3, SMALL)], axis=1)
    small_row = jnp.pad(small_row, ((0, 5), (0, 0)))
    big_row = jnp.concatenate([near[:BIG], far[:BIG]])[None, :]
    spots = jnp.concatenate([lax.dynamic_slice(pos_resize, (grid[k], 0, 0), (1, GTAB, GRID)) for k in range(4)])
    spots = spots.reshape(4 * GTAB, GRID)
    wide = ((0, 128 - 4 * GTAB), (0, 128 - GRID * GRID))
    row_table = jnp.pad(jnp.repeat(spots, GRID, axis=1), wide)
    col_table = jnp.pad(jnp.tile(spots, (1, GRID)), wide)
    tables = jnp.concatenate([lax.dynamic_slice(kernel_resize, (patch[k], 0, 0), (1, PMAX, BASE)) for k in range(4)])
    inside = jnp.arange(PMAX, dtype=jnp.int32)[None, :, None] < patch[:, None, None]
    tables = jnp.where(inside, tables, jnp.zeros_like(tables))
    return dict(
        src_col=source[:, None], src_row=source[None, :], row_at=row_at[:, None], col_at=col_at[:, None],
        row_table=row_table, col_table=col_table, tables=tables,
        big_row=big_row, big_col=big_row.T, small_row=small_row, small_col=small_row.T,
    )


def vector_rows(embed_bias, norm1_gain, norm1_bias, query_bias, value_bias, proj_bias, norm2_gain, norm2_bias, fc1_bias, fc2_bias):
    line = lambda v: v[None, :]
    return dict(
        embed_bias=line(embed_bias), norm1_gain=line(norm1_gain), norm1_bias=line(norm1_bias),
        query_bias=line(query_bias), value_bias=line(value_bias), proj_bias=line(proj_bias),
        norm2_gain=line(norm2_gain), norm2_bias=line(norm2_bias), fc1_bias=line(fc1_bias), fc2_bias=line(fc2_bias),
    )


def forward_plain(plan, vectors, pixels, wholes):
    full, wide, pair = ((SLOTS, 768), BF), ((SLOTS, 3072), BF), ((2, SLOTS, 768), BF)
    exact, square = ((SLOTS, 768), F32), ((SLOTS, SLOTS), BF)
    weights = dict(zip(WEIGHTS, wholes))
    some = lambda *keys: {k: (vectors[k] if k in vectors else plan[k]) for k in keys}

    def first(r):
        picks(r)
        resize_factors(r)
        position_weights(r)
        for ch in range(3):
            resize_channel(r, ch)
        resize_rows(r)
        for n in range(3):
            embed_tile(r, n)
        norm_forward(r.embed, r.norm1_gain, r.norm1_bias, r.hidden1)

    a = whole(
        "embed", first,
        dict(
            pixels=pixels, base_t=weights["base_t"], **constants(),
            **some("src_col", "tables", "row_at", "col_at", "row_table", "col_table"),
            **some("embed_bias", "norm1_gain", "norm1_bias"),
        ),
        dict(
            patches=wide, posw=((SLOTS, 128), BF), embed=exact, hidden1=full, w1=((4, 384, 256), BF),
            w2=((4, 768, 512), BF),
        ),
        dict(pick=square, half_big=((6, BIG, 256), BF), half_small=((6, 192, 768), BF), rest=((192, 2304), BF)),
    )
    a["hidden_far"] = from_behind(a["hidden1"], "seq", 1)

    def second(r):
        picks_back(r)
        queries(r)
        keys_values(r, 0, r.hidden1)
        keys_values(r, 1, r.hidden_far)
        attention_forward(r)
        project(r)
        norm_forward(r.middle, r.norm2_gain, r.norm2_bias, r.hidden2)
        loop(12, lambda n: feed_in(r, n))
        feed_out(r)

    b = whole(
        "block", second,
        dict(
            hidden1=a["hidden1"], hidden_far=a["hidden_far"], embed=a["embed"],
            **{k: weights[k] for k in WEIGHTS[1:]},
            **some("query_bias", "value_bias", "proj_bias", "norm2_gain", "norm2_bias", "fc1_bias", "fc2_bias"),
            **some("src_row", "big_row", "small_row"),
        ),
        dict(
            block_out=full, query=full, keys=pair, values=pair, attended=full, middle=exact, hidden2=full, act=wide,
            slope=wide,
        ),
        dict(pick_t=square, pre=((SLOTS, 256), F32)),
    )
    return dict(**a, **b, **weights)


def layer(
    pixels, patch_size, rows_first, kernel_resize, pos_resize, base_kernel, embed_bias, pos_grid, norm1_gain,
    norm1_bias, qkv_weight, query_bias, value_bias, proj_weight, proj_bias, norm2_gain, norm2_bias, fc1_weight,
    fc1_bias, fc2_weight, fc2_bias, cotangent,
):
    side = lax.axis_index("seq")
    plan = class_plan(patch_size, rows_first, pos_resize, kernel_resize, side)
    vectors = vector_rows(
        embed_bias, norm1_gain, norm1_bias, query_bias, value_bias, proj_bias, norm2_gain, norm2_bias, fc1_bias, fc2_bias
    )
    shards = shards_of(base_kernel, pos_grid, qkv_weight, proj_weight, fc1_weight, fc2_weight)
    some = lambda *keys: {k: (vectors[k] if k in vectors else plan[k] if k in plan else f[k]) for k in keys}
    full, wide, pair = ((SLOTS, 768), BF), ((SLOTS, 3072), BF), ((2, SLOTS, 768), BF)
    exact, square = ((SLOTS, 768), F32), ((SLOTS, SLOTS), BF)
    if linked():
        f = forward_linked(plan, vectors, pixels, shards)
    else:
        wholes = [lax.all_gather(member, "dp", axis=0, tiled=True) for member in shards]
        f = forward_plain(plan, vectors, pixels, wholes)

    def third(r):
        r.rows[...] = jnp.zeros((16, 768), F32)
        picks(r)
        cotangent_in(r)

        def outward(n):
            grad_fc2_tile(r, n, r.grad_fc2.at[tile(n, 256)])
            grad_pre_tile(r, n)

        loop(12, outward)
        r.hidden_t[...] = r.hidden2[...].T

        def inward(n):
            at = tile(n, 256)
            r.grad_fc1[:, at] = nn(r.hidden_t[...], r.grad_pre[:, at]).astype(BF)

        loop(12, inward)
        grad_hidden2(r)
        middle_backward(r)
        for n in range(3):
            at = pl.ds(n * 256, 256)
            r.grad_proj[at, :] = tn(r.attended[:, at], r.grad_branch[...]).astype(BF)
        attended_backward(r)
        attention_backward(r)
        far_back(r)
        bias_rows(r)

    c = whole(
        "back", third,
        dict(
            cotangent=cotangent,
            **some(
                "act", "slope", "hidden2", "middle", "attended", "query", "keys", "values", "fc2_t", "fc1_t", "proj_t",
                "qkv_t", "norm2_gain", "src_col", "big_col", "small_col",
            ),
        ),
        dict(
            grad_fc2=((3072, 768), BF), grad_fc1=((768, 3072), BF), grad_proj=((768, 768), BF), rows=((16, 768), F32),
            grad_middle=exact, grad_query=full, grad_keys=pair, grad_values=pair, far_grad=full,
        ),
        dict(
            pick=square, grad_final=full, grad_pre=wide, hidden_t=((768, SLOTS), BF), grad_norm=full,
            grad_branch=full, grad_attended=full,
        ),
    )
    far_in = from_behind(c["far_grad"], "seq", -1)

    def fourth(r):
        r.rows[...] = r.rows_in[...]
        picks_back(r)
        grad_qkv(r, lambda n: r.grad_qkv.at[:, pl.ds(n * 256, 256)])
        hidden1_backward(r)
        embed_backward(r)
        loop(12, lambda n: grad_base_tile(r, n, r.grad_base.at[tile(n, 256)]))
        small_sums(r)
        loop(6, lambda n: patches_backward(r, n))
        resize_backward(r)

    d = whole(
        "embed_back", fourth,
        dict(
            far_in=far_in, rows_in=c["rows"], grad_middle=c["grad_middle"], grad_query=c["grad_query"],
            grad_keys=c["grad_keys"], grad_values=c["grad_values"],
            **some(
                "hidden1", "hidden_far", "embed", "patches", "posw", "w1", "w2", "qkv_t", "base_t", "norm1_gain",
                "src_row",
            ),
        ),
        dict(grad_qkv=((768, 2304), BF), grad_base=((3072, 768), BF), small=((256, 768), BF), pixel_grad=((SLOTS, 6912), BF)),
        dict(
            rows=((16, 768), F32), pick_t=square, hidden_t=((768, SLOTS), BF), far_t=((768, SLOTS), BF),
            grad_norm=full, grad_embed=full, grad_patches=wide, half_big=((6, BIG, 256), BF),
            half_small=((6, 192, 768), BF), rest=((192, 2304), BF),
        ),
    )
    arrays = [c["grad_fc2"], c["grad_fc1"], c["grad_proj"], d["grad_qkv"], d["grad_base"], d["small"]]
    sums = summed_over_devices(arrays)
    grad_fc2, grad_fc1, grad_proj, grad_qkv_sum, grad_base, small = [s.astype(F32) for s in sums]
    grad_base = grad_base.reshape(3, 2, BASE, 16, 768).transpose(0, 2, 1, 3, 4).reshape(3072, 768)
    vector = lambda n: small[128 + n]
    return (
        f["block_out"], d["pixel_grad"], grad_base, vector(0), small[: GRID * GRID], vector(1), vector(2),
        grad_qkv_sum, vector(3), vector(4), grad_proj, vector(5), vector(6), vector(7), grad_fc1,
        small[136:140].reshape(-1), grad_fc2, vector(12),
    )


def solution(mesh):
    in_specs = (
        P(("dp", "seq"), None),
        P("dp"),
        P("dp"),
        P(),
        P(),
        P(None, "dp"),
        P(),
        P(None, "dp"),
        P(),
        P(),
        P(None, "dp"),
        P(),
        P(),
        P(None, "dp"),
        P(),
        P(),
        P(),
        P(None, "dp"),
        P(),
        P(None, "dp"),
        P(),
        P(("dp", "seq"), None),
    )
    out_specs = (
        P(("dp", "seq"), None),
        P(("dp", "seq"), None),
        P(),
        P(),
        P(),
        P(),
        P(),
        P(),
        P(),
        P(),
        P(),
        P(),
        P(),
        P(),
        P(),
        P(),
        P(),
        P(),
    )
    return jax.shard_map(layer, mesh=mesh, in_specs=in_specs, out_specs=out_specs, check_vma=False)
```

time: 664 us -> 491 us (0.74)
  Pallas kernels: 175 us -> 397 us
  matrix products: 188 us -> 0 us
  local copies, waits for them, and re-layouts: 109 us -> 32.1 us
  waiting for transfers between devices: 82.4 us -> 9.84 us
  other arithmetic: 57.6 us -> 30 us
  blocking collectives: 24 us -> 0 us
    pallas_call x0 -> x3, Pallas kernels: none -> 208 us  [the longest x1 124 us: call_linked(): pl.pallas_call(kernel, out_shape=[jax.ShapeDtypeStruct(s, d) for s, d, _...]
    dot_general x28 -> x0, matrix products: 174 us -> none  [the longest x1 32.1 us: body(): jnp.einsum('ncib,nia->ncab', partial_resize, resize, preferred_element_ty...]
    all_gather x5 -> x0, waiting for transfers between devices: 64.6 us -> none  [the longest x1 36 us: body(): lax.all_gather(fc2_weight, 'dp', axis=1, tiled=True)]
    convert_element_type x9 -> x0, local copies, waits for them, and re-layouts: 46.9 us -> none  [the longest x1 18.8 us: body(): pixel_grad = jnp.einsum('ncib,njb->ncij', grad_partial, resize, preferred...]
    convert_element_type x11 -> x5, other arithmetic: 43.2 us -> 17.7 us  [layer(): s.astype(F32)]
    reshape x14 -> x6, local copies, waits for them, and re-layouts: 30.3 us -> 5.77 us  [the longest x1 4.71 us: layer(): grad_base.reshape(3, 2, BASE, 16, 768).transpose(0, 2, 1, 3, 4)]
    all_gather x1 -> x0, blocking collectives: 24 us -> none  [body(): lax.all_gather(pos_grid, 'dp', axis=1, tiled=True)]
    unnamed x92 -> x29, local copies, waits for them, and re-layouts: 24.4 us -> 4.59 us
  transfers between devices with their start and end apart: 9 -> 1, of which waited for: 4 -> 1; matrix products, arithmetic and copies ran while one was open for 30% -> 0% of each run, Pallas kernels for 0% -> 0%
where the time goes in v2:
time: 491 us; the launch traced here: 486 us
  Pallas kernels  397 us (81%)
  local copies, waits for them, and re-layouts  32.1 us (7%)
  other arithmetic  30 us (6%)
  between operations  16.3 us (3%)
  waiting for transfers between devices  9.84 us (2%)
    pallas_call x1, Pallas kernels, all_sum(): pl.pallas_call(functools.partial(reduce_kernel, chunks, len(arrays)), out...  189 us
    pallas_call x1, Pallas kernels, call_linked(): pl.pallas_call(kernel, out_shape=[jax.ShapeDtypeStruct(s, d) for s, d, _...  124 us
    pallas_call x2, Pallas kernels, whole(): pl.pallas_call(kernel, out_shape=[jax.ShapeDtypeStruct(s, d) for s, d in...  84 us
    convert_element_type x5, other arithmetic, layer(): s.astype(F32)  17.7 us
    broadcast_in_dim x9, local copies, waits for them, and re-layouts, vector_rows(): line = lambda v: v[None, :]  11.4 us
    ppermute x1, waiting for transfers between devices, from_behind(): lax.ppermute(value, axis, [(i, (i + by) % peers) for i in range(peers)])  9.84 us
  transfers between devices with their start and end apart: 1, of which 1 were waited for; matrix products, arithmetic and copies ran while one was open for 0% of the time, Pallas kernels for 0%

profile of v2, /device:TPU:1, one launch (start us, length us, event | category | flops | bytes accessed | tf_op | source)
XLA Modules:
  0.0 486.2 jit_solution(1323168439469932945)
XLA Ops:
  0.7 1.4 iota_reduce_fusion
  2.0 1.4 fusion.9
  3.5 0.1 select_reduce_fusion.5
  3.6 0.7 fusion.10
  4.3 0.9 select_reduce_fusion
  5.2 0.1 iota_compare_fusion.1
  5.2 0.6 fusion.12
  10.8 0.6 fusion.11
  16.6 0.8 multiply_reduce_fusion
  17.4 0.7 broadcast_select_fusion
  18.1 0.1 slice.100
  18.2 0.1 slice.102
  18.3 0.1 pad_maximum_fusion.2
  18.4 0.1 copy.99
  18.5 0.6 pad_bitcast_fusion.refs_16_
  19.2 1.3 broadcast_in_dim.122.refs_16_.refs_15_
  20.5 1.3 broadcast_in_dim.127.refs_21_.refs_13_
  21.7 1.3 broadcast_in_dim.121.refs_15_
  23.0 1.3 broadcast_in_dim.123.refs_17_
  24.3 1.3 broadcast_in_dim.124.refs_18_
  25.5 1.3 broadcast_in_dim.125.refs_19_
  26.8 1.3 broadcast_in_dim.126.refs_20_
  28.1 1.3 broadcast_in_dim.128.refs_22_
  29.3 1.3 broadcast_in_dim.130.refs_24_
  33.2 0.8 constant_dynamic-slice_fusion.3
  34.1 0.1 reshape.163
  34.2 0.1 copy.97
  34.3 0.1 copy.98
  34.4 0.6 pad.15.refs_11_
  35.1 0.6 pad.16.refs_12_
  35.7 0.6 pad.17.clone.refs_14_
  36.3 0.8 fusion.4
  37.2 0.8 copy.104.refs_9_
  38.0 0.8 copy.105.refs_10_
  38.8 0.8 copy.103.refs_6_.refs_14_
  39.7 0.9 copy.108.refs_15_
  40.5 1.3 copy.100
  41.9 0.1 copy.101
  42.0 0.3 copy.102
  44.8 0.5 constant_dynamic-slice_fusion.7
  45.3 0.4 copy.110
  45.6 0.4 copy.112
  46.0 0.4 copy.111
  46.4 0.4 copy.113
  46.8 0.8 fusion.2.refs_26_
  47.5 0.7 maximum_select_fusion.refs_8_
  48.2 124.0 %forward.1 = (bf16[448,768]{1,0:T(8,128)(2,1)}, bf16[448,3072]{1,0:T(8,128)(2,1)}, bf16[448,128]{1,0:T(8,128)(2,1)}, f32[448,768]{1,0:T(8,128)}, bf16[448,768]{1...) custom-call(bf16[384,48]{1,0:T(8,128)(2,1)} %constant.74.clone.refs_, ...), custom_call_target="tpu_custom_call" | custom-call | tf_op jit(solution)/shard_map/forward/pallas_call | solution.py:758
  172.3 51.8 %back.1 = (bf16[3072,768]{1,0:T(8,128)(2,1)}, bf16[768,3072]{1,0:T(8,128)(2,1)}, bf16[768,768]{1,0:T(8,128)(2,1)}, f32[16,768]{1,0:T(8,128)}, f32[448,768]{1,0:T...) custom-call(bf16[448,768]{1,0:T(8,128)(2,1)} %refs_0_.2, ...), custom_call_target="tpu_custom_call" | custom-call | tf_op jit(solution)/shard_map/back/pallas_call | solution.py:933
  224.1 1.1 collective-permute-start
  225.1 9.8 %collective-permute-done.refs_0_ = bf16[448,768]{1,0:T(8,128)(2,1)S(1)} collective-permute-done((bf16[448,768]{1,0:T(8,128)(2,1)}, bf16[448,768]{1,0:T(8,128)(2,1)S(1)}, u32[]{:S(2)}, u32[]{:S(2)}) %collective-permute-start) | collective-permute-done | bytes 688160 | tf_op jit(solution)/shard_map/ppermute | solution.py:26
  234.9 0.8 copy-done.2
  235.8 32.2 %embed_back.1 = (bf16[768,2304]{1,0:T(8,128)(2,1)}, bf16[3072,768]{1,0:T(8,128)(2,1)}, bf16[256,768]{1,0:T(8,128)(2,1)}, bf16[448,6912]{1,0:T(8,128)(2,1)}) custom-call(bf16[448,768]{1,0:T(8,128)(2,1)} %copy-done.2, f32[16,768]{1,0:T(8,128)} %get-tuple-element.74.refs_1_, f32[448,768]{1,0:T(8,128)} %get-tuple-element.75.refs_2_, ...), custom_call_target="tpu_custom_call" | custom-call | tf_op jit(solution)/shard_map/embed_back/pallas_call | solution.py:933
  268.0 188.8 %shard_map.430 = (bf16[2,2,2,384,768]{4,3,2,1,0:T(8,128)(2,1)}, bf16[1,2,2,192,3072]{4,3,2,1,0:T(8,128)(2,1)}, bf16[1,2,2,192,768]{4,3,2,1,0:T(8,128)(2,1)}, bf1...) custom-call(bf16[2,2,2,384,768]{4,3,2,1,0:T(8,128)(2,1)} %bitcast.65, ...), custom_call_target="tpu_custom_call" | custom-call | tf_op jit(solution)/shard_map/pallas_call | solution.py:199
  456.8 1.0 bitcast_convert_fusion.4
  457.9 0.7 slice_reduce_fusion
  458.6 0.7 slice.115
  459.2 0.6 reshape.175
  459.9 2.8 bitcast_convert_fusion.3
  462.7 3.8 convert_bitcast_fusion
  466.5 4.7 copy.109
  471.2 3.7 bitcast_convert_fusion.2
  475.0 5.3 %bitcast_convert_fusion.1 = f32[768,3072]{1,0:T(8,128)} fusion(bf16[1,2,2,192,3072]{4,3,2,1,0:T(8,128)(2,1)S(1)} %bitcast.63), kind=kLoop, calls=%fused_computation.2 | loop fusion | flops 2359296 | bytes 14155776 | tf_op jit(solution)/shard_map/convert_element_type | solution.py:1174
  480.3 4.8 bitcast_convert_fusion
  485.1 0.8 copy.116
  (35 shorter events, 0.2 us)
Async XLA Ops:
  0.7 44.1 %copy-start = (bf16[49,48,32]{0,2,1:T(8,128)(2,1)S(1)}, bf16[49,48,32]{0,2,1:T(8,128)(2,1)}, u32[]{:S(2)}) copy-start(bf16[49,48,32]{0,2,1:T(8,128)(2,1)} %param.34) | copy-start | bytes 451588
  37.1 9.6 %copy-start.4 = (s32[448]{0:T(512)}, s32[448]{0:T(512)S(1)}, u32[]{:S(2)}) copy-start(s32[448]{0:T(512)S(1)} %get-tuple-element.134) | copy-start | bytes 5380
  37.1 9.6 %copy-start.6 = (bf16[49,48]{0,1:T(8,128)(2,1)S(1)}, bf16[49,48]{0,1:T(8,128)(2,1)}, u32[]{:S(2)}) copy-start(bf16[49,48]{0,1:T(8,128)(2,1)} %param.38) | copy-start | bytes 14116
  39.7 8.6 %copy-start.5 = (f32[512]{0:T(512)}, f32[512]{0:T(512)S(1)}, u32[]{:S(2)}) copy-start(f32[512]{0:T(512)S(1)} %pad_maximum_fusion.1) | copy-start | bytes 6148
  224.1 10.9 %collective-permute-start = (bf16[448,768]{1,0:T(8,128)(2,1)}, bf16[448,768]{1,0:T(8,128)(2,1)S(1)}, u32[]{:S(2)}, u32[]{:S(2)}) collective-permute-start(bf16[448,768]{1,0:T(8,128)(2,1)} %get-tuple-element.73), channel_id=1, source_target_pairs={{0,1},{1,0},{2,3},{3,2},{4,5},{5,4},{6,7},{7,6},{8,9},{9,8},{10,11... | collective-permute-start | bytes 2064392 | tf_op jit(solution)/shard_map/ppermute | solution.py:26
  234.9 0.9 copy-start.2
  462.7 12.3 %slice-start.2 = ((s8[4718592]{0:T(1024)(128)(4,1)}), s8[4194304]{0:T(1024)(128)(4,1)S(1)}, s32[]{:S(2)}) async-start(s8[4718592]{0:T(1024)(128)(4,1)} %bitcast.62), calls=%async_computation.2 | async-start | bytes 8388608
  466.5 4.7 copy-start.1
  466.5 8.4 %slice-start.3 = ((s8[4718592]{0:T(1024)(128)(4,1)}), s8[524288]{0:T(1024)(128)(4,1)S(1)}, s32[]{:S(2)}) async-start(s8[4718592]{0:T(1024)(128)(4,1)} %bitcast.62), calls=%async_computation.3 | async-start | bytes 1048576
  471.2 9.1 %slice-start = ((s8[4718592]{0:T(1024)(128)(4,1)}), s8[4194304]{0:T(1024)(128)(4,1)S(1)}, s32[]{:S(2)}) async-start(s8[4718592]{0:T(1024)(128)(4,1)} %bitcast.60), calls=%async_computation | async-start | bytes 8388608
  475.0 5.3 %slice-start.1 = ((s8[4718592]{0:T(1024)(128)(4,1)}), s8[524288]{0:T(1024)(128)(4,1)S(1)}, s32[]{:S(2)}) async-start(s8[4718592]{0:T(1024)(128)(4,1)} %bitcast.60), calls=%async_computation.1 | async-start | bytes 1048576
  480.3 4.8 copy-start.3
